TPU v7x, 256 devices: a whole 4x4x8 slice. The times are simulated.
256 devices in a mesh: section: 8 (over z_hi, y), expert: 32 (over x, z_lo, core).
Axes of the slice: x: 4, y: 4, z: 8 (z_hi: 2, z_lo: 4; z = z_hi * 4 + z_lo), core: 2. Of those that a mesh axis runs over, the one named last changes fastest.
Arguments:
- rising: bfloat16 [8, 2048, 3584], P('section', 'expert'), may hold values from -6 to 6
- falling: bfloat16 [8, 2048, 3584], P('section', 'expert'), may hold values from -6 to 6
- gate_up: bfloat16 [8, 2, 2, 3584, 8192], P('section', None, None, None, 'expert'), may hold values from -0.09375 to 0.09375
- down_proj: bfloat16 [8, 2, 8192, 3584], P('section', None, 'expert'), may hold values from -0.1875 to 0.1875
- norm_gains: float32 [8, 2, 3584], P('section'), may hold values from 0.25 to 1.75
- expert_ids: int32 [8, 2, 2048, 2], P('section', None, 'expert'), may hold values from 0 to 7, all different within a row; in each aligned block of 64 rows (0 to 63, 64 to 127, ..., all dimensions but the last counted through in order) at most 20 rows name the same one
- gate_values: float32 [8, 2, 2048, 2], P('section', None, 'expert'), may hold values from 0.2 to 1
Outputs:
- rising_next: bfloat16 [8, 2048, 3584], P('section', 'expert')
- falling_next: bfloat16 [8, 2048, 3584], P('section', 'expert')
Inputs may be any that keep to these rules, and one draw needn't show every extreme that they name: `expert_ids`: among the 64 tokens of one device for one section slot, no expert is chosen more than 20 times, a bound that some block reaches; a token's 2 choices differ.
All inputs are finite; a program needn't handle non-finite values.
Results may differ from a plain program's by a relative error of at most 0.0052.
Values may be sent and summed in bfloat16 or wider, within the bound.
No kernel may reach another device: no remote copies, remote signals or barrier semaphores. Data moves between devices by JAX's collectives and lax.ppermute only.
A program may use at most 128 MiB of HBM per device.

v0:
```python
import jax
import jax.numpy as jnp
from jax import lax
from jax.sharding import PartitionSpec as P

FFE = 1024
FFE_DEV = 256


EPSILON = 1e-06


def passed_along(block, axis, distance):
    devices = range(lax.axis_size(axis))
    route = [(i - distance, i) for i in devices if i - distance in devices]
    return lax.ppermute(block, axis, route)


def rms_norm(values, gain_row):
    as_float = values.astype(jnp.float32)
    scale = lax.rsqrt(jnp.mean(as_float * as_float, axis=-1, keepdims=True) + EPSILON)
    return (as_float * scale * gain_row).astype(jnp.bfloat16)


def slot_index(routes, experts, capacity):
    flat_ids = routes.reshape(-1)
    onehot = (flat_ids[:, None] == jnp.arange(experts, dtype=jnp.int32)[None, :]).astype(jnp.int32)
    position = jnp.cumsum(onehot, axis=0) - 1
    return flat_ids * capacity + jnp.sum(position * onehot, axis=1)


def dispatch_rows(normed, slot_ids, slots, top_count):
    paired = slot_ids.reshape(-1, top_count)
    one_hot = jnp.sum(
        (paired[None, :, :] == jnp.arange(slots, dtype=jnp.int32)[:, None, None]).astype(
            jnp.float32
        ),
        axis=2,
    )
    return jnp.dot(one_hot.astype(jnp.bfloat16), normed, preferred_element_type=jnp.float32).astype(
        jnp.bfloat16
    )


def body(rising, falling, gate_up, down_proj, norm_gains, expert_ids, gate_values):
    n_devices = lax.axis_size("expert")
    shards = FFE // FFE_DEV
    experts = n_devices // shards
    tok_rows = rising.shape[1]
    model_width = rising.shape[2]
    top_count = expert_ids.shape[3]
    capacity = min(tok_rows, tok_rows * top_count * 5 // (4 * experts))

    def prepare(values, member):
        normed = rms_norm(values, norm_gains[0, member])
        slot_ids = slot_index(expert_ids[0, member], experts, capacity)
        packed = dispatch_rows(normed, slot_ids, experts * capacity, top_count)
        spread = jnp.broadcast_to(
            packed.reshape(experts, 1, capacity, model_width),
            (experts, shards, capacity, model_width),
        )
        return (spread.reshape(n_devices, capacity, model_width), slot_ids)

    def expert_mlp(received, member):
        flat_rows = received.reshape(-1, model_width)
        gate_out = jnp.dot(flat_rows, gate_up[0, member, 0], preferred_element_type=jnp.float32)
        up_out = jnp.dot(flat_rows, gate_up[0, member, 1], preferred_element_type=jnp.float32)
        hidden = (jax.nn.silu(gate_out) * up_out).astype(jnp.bfloat16)
        partial_value = jnp.dot(
            hidden, down_proj[0, member], preferred_element_type=jnp.float32
        ).astype(jnp.bfloat16)
        return partial_value.reshape(received.shape)

    def finish(values, returned, slot_ids, member):
        summed = jnp.sum(
            returned.reshape(experts, shards, capacity, model_width).astype(jnp.float32), axis=1
        )
        summed = summed.reshape(experts * capacity, model_width)
        picked = jnp.take(summed, slot_ids, axis=0).reshape(tok_rows, top_count, model_width)
        mixture = jnp.sum(picked * gate_values[0, member][:, :, None], axis=1)
        return (values.astype(jnp.float32) + mixture).astype(jnp.bfloat16)

    low_in = rising[0]
    high_in = falling[0]
    low_buffer, low_slots = prepare(low_in, 0)
    high_buffer, high_slots = prepare(high_in, 1)

    def routed(buffer, member):
        return lax.all_to_all(
            expert_mlp(
                lax.all_to_all(buffer, "expert", split_axis=0, concat_axis=0, tiled=True), member
            ),
            "expert",
            split_axis=0,
            concat_axis=0,
            tiled=True,
        )

    low_back = routed(low_buffer, 0)
    high_back = routed(high_buffer, 1)
    low_out = finish(low_in, low_back, low_slots, 0)
    high_out = finish(high_in, high_back, high_slots, 1)
    from_below = passed_along(low_out, "section", 1)
    from_above = passed_along(high_out, "section", -1)
    position = lax.axis_index("section")
    final = lax.axis_size("section") - 1
    rising_next = jnp.where(position == 0, high_out, from_below)
    falling_next = jnp.where(position == final, low_out, from_above)
    return (rising_next[None], falling_next[None])


def solution(mesh):
    in_specs = (
        P("section", "expert", None),
        P("section", "expert", None),
        P("section", None, None, None, "expert"),
        P("section", None, "expert", None),
        P("section", None, None),
        P("section", None, "expert", None),
        P("section", None, "expert", None),
    )
    out_specs = (P("section", "expert", None), P("section", "expert", None))
    return jax.shard_map(body, mesh=mesh, in_specs=in_specs, out_specs=out_specs, check_vma=False)
```

profile of v0, /device:TPU:195, one launch (start us, length us, event | category | flops | bytes accessed | tf_op | source)
XLA Modules:
  0.0 586.2 jit_solution(331555382890341270)
XLA Ops:
  8.0 2.8 broadcast_in_dim.36
  10.8 7.7 %all-to-all-start = ((bf16[32,20,3584]{2,1,0:T(8,128)(2,1)}), bf16[32,20,3584]{2,1,0:T(8,128)(2,1)}, u32[]{:S(2)}, u32[]{:S(2)}) async-start(bf16[32,20,3584]{2,1,0:T(8,128)(2,1)} %bitcast.77), calls=%async_computation | async-start | bytes 11010048 | tf_op jit(solution)/shard_map/all_to_all | solution.py:91
  19.5 118.4 %all-to-all-done = bf16[32,20,3584]{2,1,0:T(8,128)(2,1)} async-done(((bf16[32,20,3584]{2,1,0:T(8,128)(2,1)}), bf16[32,20,3584]{2,1,0:T(8,128)(2,1)}, u32[]{:S(2)}, u32[]{:S(2)}) %all-to-all-start) | async-done | bytes 4587552 | tf_op jit(solution)/shard_map/all_to_all | solution.py:91
  137.9 2.8 broadcast_in_dim.38
  140.7 8.9 %all-to-all-start.2 = ((bf16[32,20,3584]{2,1,0:T(8,128)(2,1)}), bf16[32,20,3584]{2,1,0:T(8,128)(2,1)}, u32[]{:S(2)}, u32[]{:S(2)}) async-start(bf16[32,20,3584]{2,1,0:T(8,128)(2,1)} %bitcast.78), calls=%async_computation.2 | async-start | bytes 11010048 | tf_op jit(solution)/shard_map/all_to_all | solution.py:91
  149.6 7.3 %reshape.100 = bf16[640,3584]{1,0:T(8,128)(2,1)} reshape(bf16[32,20,3584]{2,1,0:T(8,128)(2,1)} %all-to-all-done) | data formatting | bytes 9175040 | tf_op jit(solution)/shard_map/reshape | solution.py:65
  156.9 4.2 fusion.8
  161.1 10.4 %convolution_convert_fusion.1 = bf16[640,3584]{1,0:T(8,128)(2,1)} fusion(bf16[1,2,256,3584]{3,2,1,0:T(8,128)(2,1)} %param.12, bf16[640,3584]{1,0:T(8,128)(2,1)} %reshape.100, bf16[1,2,2,3584,256]{4,3,2,1,0:T(8,128)(2,1)} %param.11, f32[640,256]{1,0:T(8,128)S(1)} %fusion.8), kind=kOutput, calls=%fused_computation.5 | convolution fusion | flops 2352087040 | bytes 13500416 | tf_op jit(solution)/shard_map/dot_general | solution.py:69
  171.5 7.3 %reshape.101 = bf16[32,20,3584]{2,1,0:T(8,128)(2,1)} reshape(bf16[640,3584]{1,0:T(8,128)(2,1)} %convolution_convert_fusion.1) | data formatting | bytes 9175040 | tf_op jit(solution)/shard_map/reshape | solution.py:72
  178.7 90.2 %all-to-all-done.2 = bf16[32,20,3584]{2,1,0:T(8,128)(2,1)} async-done(((bf16[32,20,3584]{2,1,0:T(8,128)(2,1)}), bf16[32,20,3584]{2,1,0:T(8,128)(2,1)}, u32[]{:S(2)}, u32[]{:S(2)}) %all-to-all-start.2) | async-done | bytes 4587552 | tf_op jit(solution)/shard_map/all_to_all | solution.py:91
  269.0 9.0 %all-to-all-start.1 = ((bf16[32,20,3584]{2,1,0:T(8,128)(2,1)}), bf16[32,20,3584]{2,1,0:T(8,128)(2,1)}, u32[]{:S(2)}, u32[]{:S(2)}) async-start(bf16[32,20,3584]{2,1,0:T(8,128)(2,1)} %reshape.101), calls=%async_computation.1 | async-start | bytes 11010048 | tf_op jit(solution)/shard_map/all_to_all | solution.py:89
  278.0 7.3 %reshape.105 = bf16[640,3584]{1,0:T(8,128)(2,1)} reshape(bf16[32,20,3584]{2,1,0:T(8,128)(2,1)} %all-to-all-done.2) | data formatting | bytes 9175040 | tf_op jit(solution)/shard_map/reshape | solution.py:65
  285.3 4.2 fusion.3
  289.5 10.4 %convolution_convert_fusion = bf16[640,3584]{1,0:T(8,128)(2,1)} fusion(bf16[1,2,256,3584]{3,2,1,0:T(8,128)(2,1)} %param.12, bf16[640,3584]{1,0:T(8,128)(2,1)} %reshape.105, bf16[1,2,2,3584,256]{4,3,2,1,0:T(8,128)(2,1)} %param.11, f32[640,256]{1,0:T(8,128)S(1)} %fusion.3), kind=kOutput, calls=%fused_computation.4 | convolution fusion | flops 2352087040 | bytes 13500416 | tf_op jit(solution)/shard_map/dot_general | solution.py:69
  299.9 7.2 %reshape.106 = bf16[32,20,3584]{2,1,0:T(8,128)(2,1)} reshape(bf16[640,3584]{1,0:T(8,128)(2,1)} %convolution_convert_fusion) | data formatting | bytes 9175040 | tf_op jit(solution)/shard_map/reshape | solution.py:72
  307.1 90.3 %all-to-all-done.1 = bf16[32,20,3584]{2,1,0:T(8,128)(2,1)} async-done(((bf16[32,20,3584]{2,1,0:T(8,128)(2,1)}), bf16[32,20,3584]{2,1,0:T(8,128)(2,1)}, u32[]{:S(2)}, u32[]{:S(2)}) %all-to-all-start.1) | async-done | bytes 4587552 | tf_op jit(solution)/shard_map/all_to_all | solution.py:89
  397.4 9.0 %all-to-all-start.3 = ((bf16[32,20,3584]{2,1,0:T(8,128)(2,1)}), bf16[32,20,3584]{2,1,0:T(8,128)(2,1)}, u32[]{:S(2)}, u32[]{:S(2)}) async-start(bf16[32,20,3584]{2,1,0:T(8,128)(2,1)} %reshape.106), calls=%async_computation.3 | async-start | bytes 11010048 | tf_op jit(solution)/shard_map/all_to_all | solution.py:89
  406.7 5.3 convert_reduce_fusion.1
  420.3 4.1 multiply_reduce_fusion.1
  424.5 5.7 collective-permute-start.1
  430.3 105.3 %all-to-all-done.3 = bf16[32,20,3584]{2,1,0:T(8,128)(2,1)} async-done(((bf16[32,20,3584]{2,1,0:T(8,128)(2,1)}), bf16[32,20,3584]{2,1,0:T(8,128)(2,1)}, u32[]{:S(2)}, u32[]{:S(2)}) %all-to-all-start.3) | async-done | bytes 4587552 | tf_op jit(solution)/shard_map/all_to_all | solution.py:89
  535.6 5.3 convert_reduce_fusion
  549.3 4.1 multiply_reduce_fusion
  557.3 28.1 %collective-permute-done = bf16[64,3584]{1,0:T(8,128)(2,1)S(1)} collective-permute-done((bf16[64,3584]{1,0:T(8,128)(2,1)S(1)}, bf16[64,3584]{1,0:T(8,128)(2,1)S(1)}, u32[]{:S(2)}, u32[]{:S(2)}) %collective-permute-start) | collective-permute-done | bytes 458784 | tf_op jit(solution)/shard_map/ppermute | solution.py:16
  (52 shorter events, 30.0 us)
Async XLA Ops:
  10.8 7.8 %copy-start.1 = (bf16[1,64,3584]{2,1,0:T(8,128)(2,1)S(1)}, bf16[1,64,3584]{2,1,0:T(8,128)(2,1)}, u32[]{:S(2)}) copy-start(bf16[1,64,3584]{2,1,0:T(8,128)(2,1)} %param.9) | copy-start | bytes 1376260
  10.8 127.1 %all-to-all-start = ((bf16[32,20,3584]{2,1,0:T(8,128)(2,1)}), bf16[32,20,3584]{2,1,0:T(8,128)(2,1)}, u32[]{:S(2)}, u32[]{:S(2)}) async-start(bf16[32,20,3584]{2,1,0:T(8,128)(2,1)} %bitcast.77), calls=%async_computation | async-start | bytes 11010048 | tf_op jit(solution)/shard_map/all_to_all | solution.py:91
  140.7 128.3 %all-to-all-start.2 = ((bf16[32,20,3584]{2,1,0:T(8,128)(2,1)}), bf16[32,20,3584]{2,1,0:T(8,128)(2,1)}, u32[]{:S(2)}, u32[]{:S(2)}) async-start(bf16[32,20,3584]{2,1,0:T(8,128)(2,1)} %bitcast.78), calls=%async_computation.2 | async-start | bytes 11010048 | tf_op jit(solution)/shard_map/all_to_all | solution.py:91
  269.0 128.4 %all-to-all-start.1 = ((bf16[32,20,3584]{2,1,0:T(8,128)(2,1)}), bf16[32,20,3584]{2,1,0:T(8,128)(2,1)}, u32[]{:S(2)}, u32[]{:S(2)}) async-start(bf16[32,20,3584]{2,1,0:T(8,128)(2,1)} %reshape.101), calls=%async_computation.1 | async-start | bytes 11010048 | tf_op jit(solution)/shard_map/all_to_all | solution.py:89
  307.1 99.3 %copy-start.2 = (f32[1,2,64,2]{2,3,1,0:T(2,128)S(1)}, f32[1,2,64,2]{2,3,1,0:T(2,128)}, u32[]{:S(2)}) copy-start(f32[1,2,64,2]{2,3,1,0:T(2,128)} %param.15) | copy-start | bytes 3076
  397.4 138.2 %all-to-all-start.3 = ((bf16[32,20,3584]{2,1,0:T(8,128)(2,1)}), bf16[32,20,3584]{2,1,0:T(8,128)(2,1)}, u32[]{:S(2)}, u32[]{:S(2)}) async-start(bf16[32,20,3584]{2,1,0:T(8,128)(2,1)} %reshape.106), calls=%async_computation.3 | async-start | bytes 11010048 | tf_op jit(solution)/shard_map/all_to_all | solution.py:89
  418.0 6.4 %copy-start = (bf16[1,64,3584]{2,1,0:T(8,128)(2,1)S(1)}, bf16[1,64,3584]{2,1,0:T(8,128)(2,1)}, u32[]{:S(2)}) copy-start(bf16[1,64,3584]{2,1,0:T(8,128)(2,1)} %param.10) | copy-start | bytes 1376260
  424.5 128.9 %collective-permute-start.1 = (bf16[64,3584]{1,0:T(8,128)(2,1)S(1)}, bf16[64,3584]{1,0:T(8,128)(2,1)}, u32[]{:S(2)}, u32[]{:S(2)}) collective-permute-start(bf16[64,3584]{1,0:T(8,128)(2,1)S(1)} %fusion.35), channel_id=1, source_target_pairs={{32,0},{64,32},{96,64},{128,96},{160,128},{192,160},{224,192},{33,... | collective-permute-start | bytes 1376264 | tf_op jit(solution)/shard_map/ppermute | solution.py:16
  555.4 30.1 %collective-permute-start = (bf16[64,3584]{1,0:T(8,128)(2,1)S(1)}, bf16[64,3584]{1,0:T(8,128)(2,1)S(1)}, u32[]{:S(2)}, u32[]{:S(2)}) collective-permute-start(bf16[64,3584]{1,0:T(8,128)(2,1)S(1)} %get-tuple-element.6), channel_id=1, source_target_pairs={{0,32},{32,64},{64,96},{96,128},{128,160},{160,192},{192,224},{1,3... | collective-permute-start | bytes 1376264 | tf_op jit(solution)/shard_map/ppermute | solution.py:16
where the time goes:
time: 588 us; the launch traced here: 586 us
  waiting for transfers between devices  432 us (73%)
  local copies, waits for them, and re-layouts  51.2 us (9%)
  starting transfers between devices  42.3 us (7%)
  matrix products  31.3 us (5%)
  other arithmetic  28.2 us (5%)
    all_to_all x2, waiting for transfers between devices, routed(): lax.all_to_all(buffer, 'expert', split_axis=0, concat_axis=0, tiled=True)  209 us
    all_to_all x2, waiting for transfers between devices, routed(): lax.all_to_all(expert_mlp(lax.all_to_all(buffer, 'expert', split_axis=0,...  196 us
    ppermute x2, waiting for transfers between devices, passed_along(): return lax.ppermute(block, axis, route)  28.1 us
    dot_general x2, matrix products, expert_mlp(): jnp.dot(hidden, down_proj[0, member], preferred_element_type=jnp.float32)  20.7 us
    all_to_all x2, starting transfers between devices, routed(): lax.all_to_all(expert_mlp(lax.all_to_all(buffer, 'expert', split_axis=0,...  18 us
    all_to_all x2, starting transfers between devices, routed(): lax.all_to_all(buffer, 'expert', split_axis=0, concat_axis=0, tiled=True)  16.7 us
    reshape x2, local copies, waits for them, and re-layouts, expert_mlp(): return partial_value.reshape(received.shape)  14.5 us
    reshape x2, local copies, waits for them, and re-layouts, expert_mlp(): flat_rows = received.reshape(-1, model_width)  14.5 us
  transfers between devices with their start and end apart: 6, of which 5 were waited for; matrix products, arithmetic and copies ran while one was open for 16% of the time, Pallas kernels for 0%

commit v1 on v0

v1 whole, which is shorter than its diff:
```python
import jax
import jax.numpy as jnp
from jax import lax
from jax.experimental import pallas as pl
from jax.experimental.pallas import tpu as pltpu
from jax.sharding import PartitionSpec as P

EPSILON = 1e-06
X, Z, C = 4, 4, 2
CAP = 20
STRIDE = 48
FACTS = 128
UP_TILE, DOWN_TILE = 1792, 1792
PIECE = 512
HALVES = 2


def moved(block, place):
    route = []
    for x in range(X):
        for z in range(Z):
            for c in range(C):
                tx, tz, tc = place(x, z, c)
                route.append(((x * Z + z) * C + c, ((tx % X) * Z + tz) * C + tc))
    return lax.ppermute(block, "expert", route)


def along_x(block, k):
    return moved(block, lambda x, z, c: (x + k, z, c))


def across_z(block, k):
    return moved(block, lambda x, z, c: (x, z ^ k, c))


def across_cores(block):
    return moved(block, lambda x, z, c: (x, z, 1 - c))


def shifted(block, distance):
    devices = range(lax.axis_size("section"))
    route = [(i, i + distance) for i in devices if i + distance in devices]
    return lax.ppermute(block, "section", route)


def after(value, *others):
    return lax.optimization_barrier((value, *others))[0]


def plus(a, b):
    return (a.astype(jnp.float32) + b.astype(jnp.float32)).astype(jnp.bfloat16)


def call(kernel, out_shape, **kw):
    return pl.pallas_call(
        kernel,
        out_shape=out_shape,
        cost_estimate=pl.CostEstimate(flops=1000, bytes_accessed=1000, transcendentals=0),
        compiler_params=pltpu.CompilerParams(vmem_limit_bytes=60 * 1024 * 1024),
        **kw,
    )


def shaped(*shape, kind=jnp.bfloat16):
    return jax.ShapeDtypeStruct(shape, kind)


def iota(shape, dim):
    return lax.broadcasted_iota(jnp.int32, shape, dim)


def dot(a, b, contract=((1,), (0,))):
    return lax.dot_general(a, b, (contract, ((), ())), preferred_element_type=jnp.float32)


def pieces(width):
    return [slice(at, min(at + PIECE, width)) for at in range(0, width, PIECE)]


def normed_of(x, gain):
    x = x.astype(jnp.float32)
    scale = lax.rsqrt(jnp.mean(x * x, axis=-1, keepdims=True) + EPSILON)
    return (x * scale * gain).astype(jnp.bfloat16)


def packed(ids, gates):
    rows = [ids[r : r + 1].astype(jnp.float32) for r in range(2)]
    rest = [gates[r : r + 1] for r in range(2)]
    for _ in range(3):
        terms = [g.astype(jnp.bfloat16).astype(jnp.float32) for g in rest]
        rest = [g - t for g, t in zip(rest, terms)]
        rows += terms
    shape = (8, ids.shape[1])
    total = jnp.zeros(shape, jnp.float32)
    for n, row in enumerate(rows):
        total = jnp.where(iota(shape, 0) == n, jnp.broadcast_to(row, shape), total)
    unit = jnp.where(iota((8, FACTS), 0) == iota((8, FACTS), 1), 1.0, 0.0).astype(jnp.bfloat16)
    return dot(total.astype(jnp.bfloat16), unit, ((0,), (0,))).astype(jnp.bfloat16)


def unpacked(block):
    unit = jnp.where(iota((8, FACTS), 0) == iota((8, FACTS), 1), 1.0, 0.0).astype(jnp.bfloat16)
    rows = dot(unit, block, ((1,), (1,)))
    return [rows[r : r + 1] for r in range(2)] + [
        rows[2 + r : 3 + r] + rows[4 + r : 5 + r] + rows[6 + r : 7 + r] for r in range(2)
    ]


def routes(facts, group, capacity, stride, hot_ref, high_ref, low_ref):
    tokens = facts[0].shape[1]
    count = group * X
    place = lax.axis_index("expert")
    x, half = place // (Z * C), place // (2 * C) % 2
    row = iota((count, tokens), 0)
    if group == 1:
        mine = ((x + row) & (X - 1)) * 2 + half
    else:
        mine = ((x + (row >> 1)) & (X - 1)) * 2 + ((half + row) & 1)
    mine = mine.astype(jnp.float32)
    first, second = facts[0] == mine, facts[1] == mine
    gate = jnp.where(first, facts[2], 0.0) + jnp.where(second, facts[3], 0.0)
    match = jnp.where(first, 1.0, 0.0) + jnp.where(second, 1.0, 0.0)
    until = iota((tokens, tokens), 0) <= iota((tokens, tokens), 1)
    rank = dot(match.astype(jnp.bfloat16), jnp.where(until, 1.0, 0.0).astype(jnp.bfloat16))
    rank = jnp.where(match > 0.0, rank, 0.0)
    shape = (stride, tokens)
    row = iota(shape, 0)
    for k in range(X):
        wanted, weight, slot = (
            jnp.broadcast_to(rank[k * group : k * group + 1], shape),
            jnp.broadcast_to(gate[k * group : k * group + 1], shape),
            row,
        )
        for q in range(1, group):
            e, later = k * group + q, row >= q * capacity
            wanted = jnp.where(later, jnp.broadcast_to(rank[e : e + 1], shape), wanted)
            weight = jnp.where(later, jnp.broadcast_to(gate[e : e + 1], shape), weight)
            slot = jnp.where(later, row - q * capacity, slot)
        slot = jnp.where(row < group * capacity, slot + 1, -1)
        here = wanted == slot.astype(jnp.float32)
        weight = jnp.where(here, weight, 0.0)
        high = weight.astype(jnp.bfloat16)
        at = slice(k * stride, (k + 1) * stride)
        hot_ref[at] = jnp.where(here, 1.0, 0.0).astype(jnp.bfloat16)
        high_ref[at] = high
        low_ref[at] = (weight - high.astype(jnp.float32)).astype(jnp.bfloat16)


def norm_line(values, gains, ids, gates, slot):
    _, rows, width = values.shape

    def kernel(x_ref, gain_ref, ids_ref, gates_ref, out):
        out[:, :width] = normed_of(x_ref[0], gain_ref[0, slot : slot + 1])
        out[:, width:] = packed(ids_ref[0, slot], gates_ref[0, slot])

    return call(kernel, shaped(rows, width + FACTS))(values, gains, ids, gates)


def dispatch_own(values, gains, ids, gates, slot):
    _, rows, width = values.shape

    def kernel(x_ref, gain_ref, ids_ref, gates_ref, *refs):
        outs, (high, low, hot, held) = refs[:X], refs[X:]
        facts = [ids_ref[0, slot, r : r + 1].astype(jnp.float32) for r in range(2)]
        facts += [gates_ref[0, slot, r : r + 1] for r in range(2)]
        routes(facts, 2, CAP, STRIDE, hot, high, low)
        held[...] = normed_of(x_ref[0], gain_ref[0, slot : slot + 1])
        for at in pieces(width):
            value = dot(hot[...], held[:, at]).astype(jnp.bfloat16)
            for k in range(X):
                outs[k][:, at] = value[k * STRIDE : k * STRIDE + 2 * CAP]

    return call(
        kernel,
        [shaped(2 * CAP, width)] * X + [shaped(X * STRIDE, rows)] * 2,
        scratch_shapes=[
            pltpu.VMEM((X * STRIDE, rows), jnp.bfloat16),
            pltpu.VMEM((rows, width), jnp.bfloat16),
        ],
    )(values, gains, ids, gates)


def dispatch_line(blocks):
    rows, width = blocks[0].shape[0], blocks[0].shape[1] - FACTS
    tokens, slots = Z * rows, Z * CAP

    def kernel(*refs):
        ins, outs, (high, low, hot, held) = refs[:Z], refs[Z : Z + X], refs[Z + X :]
        for n in range(Z):
            held[n * rows : (n + 1) * rows] = ins[n][...]
        routes(unpacked(held[:, width:]), 1, slots, slots, hot, high, low)
        for at in pieces(width):
            value = dot(hot[...], held[:, at]).astype(jnp.bfloat16)
            for k in range(X):
                outs[k][:, at] = value[k * slots : (k + 1) * slots]

    return call(
        kernel,
        [shaped(slots, width)] * X + [shaped(X * slots, tokens)] * 2,
        scratch_shapes=[
            pltpu.VMEM((X * slots, tokens), jnp.bfloat16),
            pltpu.VMEM((tokens, width + FACTS), jnp.bfloat16),
        ],
    )(*blocks)


def moves(shape, spans):
    row, column = iota(shape, 0), iota(shape, 1)
    wanted = jnp.full(shape, -1, jnp.int32)
    for to, of, rows in spans:
        wanted = jnp.where((row >= to) & (row < to + rows), row - to + of, wanted)
    return jnp.where(wanted == column, 1.0, 0.0).astype(jnp.bfloat16)


def by_half(blocks):
    slots, width = blocks[0].shape
    half = X * CAP
    spans = [(q * half + k * CAP, k * STRIDE + q * CAP, CAP) for q in range(2) for k in range(X)]

    def kernel(*refs):
        ins, outs, held = refs[:X], refs[X : X + 2], refs[X + 2]
        held[...] = jnp.zeros_like(held)
        for k in range(X):
            held[k * STRIDE : k * STRIDE + slots] = ins[k][...]
        take = moves((2 * half, X * STRIDE), spans)
        for at in pieces(width):
            value = dot(take, held[:, at]).astype(jnp.bfloat16)
            for q in range(2):
                outs[q][:, at] = value[q * half : (q + 1) * half]

    return call(
        kernel,
        [shaped(half, width)] * 2,
        scratch_shapes=[pltpu.VMEM((X * STRIDE, width), jnp.bfloat16)],
    )(*blocks)


def by_column(near, side, far):
    half, width = near.shape
    spans = [(k * STRIDE + q * CAP, q * half + k * CAP, CAP) for q in range(2) for k in range(X)]

    def kernel(near_ref, side_ref, far_ref, *refs):
        outs, held = refs[:X], refs[X]
        held[:half] = plus(near_ref[...], side_ref[...])
        held[half:] = far_ref[...]
        take = moves((X * STRIDE, 2 * half), spans)
        for at in pieces(width):
            value = dot(take, held[:, at]).astype(jnp.bfloat16)
            for k in range(X):
                outs[k][:, at] = value[k * STRIDE : k * STRIDE + 2 * CAP]

    return call(
        kernel,
        [shaped(2 * CAP, width)] * X,
        scratch_shapes=[pltpu.VMEM((2 * half, width), jnp.bfloat16)],
    )(near, side, far)


def experts(blocks, own, own_down, peer, peer_down, slot):
    slots, width = blocks[0].shape
    units = own.shape[4]
    rows = X * slots
    steps, down_steps = width // UP_TILE, width // DOWN_TILE

    def kernel(*refs):
        ins, ups, downs, outs = refs[:X], refs[X : X + 4], refs[X + 4 : X + 6], refs[X + 6 : 2 * X + 6]
        held, acc, hidden = refs[2 * X + 6 :]
        step = pl.program_id(0)

        @pl.when(step < steps)
        def _():
            for k in range(X):
                held[k * slots : (k + 1) * slots] = ins[k][...]
            weight = jnp.concatenate([u[0, 0, 0] for u in ups], axis=1)
            value = dot(held[...], weight)

            @pl.when(step == 0)
            def _():
                acc[...] = value

            @pl.when(step > 0)
            def _():
                acc[...] += value

        @pl.when(step == steps - 1)
        def _():
            for n in range(C):
                gate = acc[:, 2 * n * units : (2 * n + 1) * units]
                value = gate / (1.0 + jnp.exp(-gate)) * acc[:, (2 * n + 1) * units : (2 * n + 2) * units]
                hidden[:, n * units : (n + 1) * units] = value.astype(jnp.bfloat16)

        @pl.when(step >= steps)
        def _():
            weight = jnp.concatenate([d[0, 0] for d in downs], axis=0)
            value = dot(hidden[...], weight).astype(jnp.bfloat16)
            for k in range(X):
                outs[k][...] = value[k * slots : (k + 1) * slots]

    def into(s):
        return jnp.minimum(s, steps - 1)

    def out_of(s):
        return jnp.maximum(s - steps, 0)

    def up(which):
        return pl.BlockSpec((1, 1, 1, UP_TILE, units), lambda s: (0, slot, which, into(s), 0))

    down = pl.BlockSpec((1, 1, units, DOWN_TILE), lambda s: (0, slot, 0, out_of(s)))
    return call(
        kernel,
        [shaped(slots, width)] * X,
        grid=(steps + down_steps,),
        in_specs=[pl.BlockSpec((slots, UP_TILE), lambda s: (0, into(s)))] * X
        + [up(0), up(1), up(0), up(1), down, down],
        out_specs=[pl.BlockSpec((slots, DOWN_TILE), lambda s: (0, out_of(s)))] * X,
        scratch_shapes=[
            pltpu.VMEM((rows, UP_TILE), jnp.bfloat16),
            pltpu.VMEM((rows, 2 * C * units), jnp.float32),
            pltpu.VMEM((rows, C * units), jnp.bfloat16),
        ],
    )(*blocks, own, own, peer, peer, own_down, peer_down)


def combine_own(high, low, blocks, values):
    slots, width = blocks[0].shape
    tokens = high.shape[1]

    def kernel(high_ref, low_ref, *refs):
        ins, x_ref, out, held = refs[:X], refs[X], refs[X + 1], refs[X + 2]
        held[...] = jnp.zeros_like(held)
        for k in range(X):
            held[k * STRIDE : k * STRIDE + slots] = ins[k][...]
        for at in pieces(width):
            mixture = dot(high_ref[...], held[:, at], ((0,), (0,)))
            mixture += dot(low_ref[...], held[:, at], ((0,), (0,)))
            out[:, at] = (x_ref[0, :, at].astype(jnp.float32) + mixture).astype(jnp.bfloat16)

    return call(
        kernel,
        shaped(tokens, width),
        scratch_shapes=[pltpu.VMEM((X * STRIDE, width), jnp.bfloat16)],
    )(high, low, *blocks, values)


def combine_line(high, low, blocks):
    slots, width = blocks[0].shape
    tokens = high.shape[1]
    rows, part = tokens // Z, width // HALVES

    def kernel(high_ref, low_ref, *refs):
        ins, keep, send, held = refs[:X], refs[X : X + 2 * HALVES], refs[-3:-1], refs[-1]
        for k in range(X):
            held[k * slots : (k + 1) * slots] = ins[k][...]
        for h in range(HALVES):
            for at in pieces(part):
                there = slice(h * part + at.start, h * part + at.stop)
                total = dot(high_ref[...], held[:, there], ((0,), (0,)))
                total += dot(low_ref[...], held[:, there], ((0,), (0,)))
                for n in range(2):
                    keep[2 * h + n][:, at] = total[n * rows : (n + 1) * rows]
                    lower = slice((2 + n) * rows, (3 + n) * rows)
                    send[n][:, there] = total[lower].astype(jnp.bfloat16)

    *keep, side, corner = call(
        kernel,
        [shaped(rows, part, kind=jnp.float32)] * (2 * HALVES) + [shaped(rows, width)] * 2,
        scratch_shapes=[pltpu.VMEM((X * slots, width), jnp.bfloat16)],
    )(high, low, *blocks)
    return keep[::2], keep[1::2], side, corner


def body(rising, falling, gate_up, down_proj, norm_gains, expert_ids, gate_values):
    ids, gates = (jnp.transpose(a, (0, 1, 3, 2)) for a in (expert_ids, gate_values))

    normed = norm_line(falling, norm_gains, ids, gates, 1)
    side, far = across_z(normed, 1), across_z(normed, 2)
    peer_up = across_cores(gate_up)
    *own, own_high, own_low = dispatch_own(rising, after(norm_gains, normed), ids, gates, 0)
    own[2] = after(own[2], peer_up)
    own = [own[0]] + [along_x(own[k], k) for k in range(1, X)]
    far = after(far, own[0])
    corner = across_z(far, 1)
    own[0] = after(own[0], far, side)
    near0, far0 = by_half(own)
    peer_down = across_cores(after(down_proj, near0))
    far0 = across_z(after(far0, corner), 2)
    side0 = across_z(after(near0, corner), 1)

    *line, line_high, line_low = dispatch_line([normed, far, side, after(corner, peer_down)])
    far0 = after(far0, line[0], side0)
    rows0 = [near0, far0, side0, across_z(far0, 1)]
    rows1 = [line[0]] + [along_x(line[k], k) for k in range(1, X)]

    line = experts(rows1, gate_up, down_proj, peer_up, peer_down, 1)
    rows0[0] = after(rows0[0], line[0])
    line = [line[0]] + [along_x(line[k], -k) for k in range(1, X)]
    near0, far0, side0, corner0 = experts(rows0, gate_up, down_proj, peer_up, peer_down, 0)
    corner0, side0 = across_z(corner0, 1), across_z(side0, 1)
    near1, far1, side1, corner1 = combine_line(line_high, line_low, line)
    far0 = across_z(plus(far0, after(corner0, near1[0], side0)), 2)
    corner1, side1 = across_z(corner1, 1), across_z(side1, 1)
    width = falling.shape[2] // HALVES
    part = [slice(h * width, (h + 1) * width) for h in range(HALVES)]
    sent1 = [plus(far1[h], corner1[:, part[h]]) for h in range(HALVES)]
    own = by_column(after(near0, sent1[0]), side0, far0)
    own = [own[0]] + [along_x(own[k], -k) for k in range(1, X)]
    far1 = [across_z(sent1[0], 2)]
    far1[0] = after(far1[0], own[0])

    def ended(h):
        mixture = near1[h] + (side1[:, part[h]].astype(jnp.float32) + far1[h].astype(jnp.float32))
        return plus(falling[0, :, part[h]], mixture)

    far1.append(across_z(after(sent1[1], far1[0]), 2))
    out1 = [ended(0)]
    got1 = [shifted(out1[0], -1)]
    own[0] = after(own[0], out1[0])
    out0 = combine_own(own_high, own_low, own, rising)
    got0 = shifted(out0, 1)
    far1[1] = after(far1[1], out0)
    out1.append(ended(1))
    got1.append(shifted(out1[1], -1))
    got1[0] = after(got1[0], got0)
    out1, got1 = jnp.concatenate(out1, axis=1), jnp.concatenate(got1, axis=1)
    position = lax.axis_index("section")
    final = lax.axis_size("section") - 1
    rising_next = jnp.where(position == 0, out1, got0)
    falling_next = jnp.where(position == final, out0, got1)
    return (rising_next[None], falling_next[None])


def solution(mesh):
    in_specs = (
        P("section", "expert", None),
        P("section", "expert", None),
        P("section", None, None, None, "expert"),
        P("section", None, "expert", None),
        P("section", None, None),
        P("section", None, "expert", None),
        P("section", None, "expert", None),
    )
    out_specs = (P("section", "expert", None), P("section", "expert", None))
    return jax.shard_map(body, mesh=mesh, in_specs=in_specs, out_specs=out_specs, check_vma=False)
```

time: 588 us -> 210 us (0.36)
  waiting for transfers between devices: 432 us -> 107 us
  local copies, waits for them, and re-layouts: 51.2 us -> 4.07 us
  Pallas kernels: 0 us -> 42.2 us
  matrix products: 31.3 us -> 0 us
  other arithmetic: 28.2 us -> 6.11 us
    all_to_all x4 -> x0, waiting for transfers between devices: 404 us -> none  [the longest x2 209 us: routed(): lax.all_to_all(buffer, 'expert', split_axis=0, concat_axis=0, tiled=True)]
    ppermute x2 -> x30, waiting for transfers between devices: 28.1 us -> 107 us  [the longest x27 90.4 us: moved(): return lax.ppermute(block, 'expert', route)]
    pallas_call x0 -> x9, Pallas kernels: none -> 42.2 us  [the longest x2 18.8 us: experts(): call(kernel, [shaped(slots, width)] * X, grid=(steps + down_steps,), in_s...]
    ppermute x2 -> x30, starting transfers between devices: 7.65 us -> 46.2 us  [the longest x27 30.1 us: moved(): return lax.ppermute(block, 'expert', route)]
    reshape x8 -> x0, local copies, waits for them, and re-layouts: 37.5 us -> none  [the longest x2 14.5 us: expert_mlp(): return partial_value.reshape(received.shape)]
    all_to_all x4 -> x0, starting transfers between devices: 34.7 us -> none  [the longest x2 18 us: routed(): lax.all_to_all(expert_mlp(lax.all_to_all(buffer, 'expert', split_axis=0,...]
    dot_general x6 -> x0, matrix products: 31.3 us -> none  [the longest x2 20.7 us: expert_mlp(): jnp.dot(hidden, down_proj[0, member], preferred_element_type=jnp.float32)]
    reduce_sum x9 -> x0, other arithmetic: 20.6 us -> none  [the longest x2 10.6 us: finish(): jnp.sum(returned.reshape(experts, shards, capacity, model_width).astype(j...]
  transfers between devices with their start and end apart: 6 -> 30, of which waited for: 5 -> 13; matrix products, arithmetic and copies ran while one was open for 16% -> 3% of each run, Pallas kernels for 0% -> 19%
where the time goes in v1:
time: 210 us; the launch traced here: 207 us
  waiting for transfers between devices  107 us (51%)
  starting transfers between devices  46.2 us (22%)
  Pallas kernels  42.2 us (20%)
  other arithmetic  6.11 us (3%)
  local copies, waits for them, and re-layouts  4.07 us (2%)
    ppermute x27, waiting for transfers between devices, moved(): return lax.ppermute(block, 'expert', route)  90.4 us
    ppermute x27, starting transfers between devices, moved(): return lax.ppermute(block, 'expert', route)  30.1 us
    pallas_call x2, Pallas kernels, experts(): call(kernel, [shaped(slots, width)] * X, grid=(steps + down_steps,), in_s...  18.8 us
    ppermute x3, waiting for transfers between devices, shifted(): return lax.ppermute(block, 'section', route)  16.8 us
    ppermute x3, starting transfers between devices, shifted(): return lax.ppermute(block, 'section', route)  16.2 us
    pallas_call x1, Pallas kernels, dispatch_line(): call(kernel, [shaped(slots, width)] * X + [shaped(X * slots, tokens)] * 2...  5.18 us
    pallas_call x1, Pallas kernels, combine_line(): call(kernel, [shaped(rows, part, kind=jnp.float32)] * (2 * HALVES) + [sha...  5.05 us
    convert_element_type x4, other arithmetic, plus(): return (a.astype(jnp.float32) + b.astype(jnp.float32)).astype(jnp.bfloat16)  4.35 us
  transfers between devices with their start and end apart: 30, of which 13 were waited for; matrix products, arithmetic and copies ran while one was open for 3% of the time, Pallas kernels for 19%

profile of v1, /device:TPU:195, one launch (start us, length us, event | category | flops | bytes accessed | tf_op | source)
XLA Modules:
  0.0 206.7 jit_solution(15224790526615142065)
XLA Ops:
  1.4 2.1 shard_map.86.refs_0_
  5.4 2.7 %shard_map.87 = (bf16[40,3584]{1,0:T(8,128)(2,1)}, bf16[40,3584]{1,0:T(8,128)(2,1)}, bf16[40,3584]{1,0:T(8,128)(2,1)}, bf16[40,3584]{1,0:T(8,128)(2,1)}, bf16[19...) custom-call(bf16[1,64,3584]{2,1,0:T(8,128)(2,1)} %refs_4_.5, f32[1,2,3584]{2,1,0:T(2,128)} %gain_ref.2, ...), custom_call_target="tpu_custom_call" | custom-call | flops 1000 | bytes 1000 | tf_op jit(solution)/shard_map/pallas_call | solution.py:173
  9.5 3.5 %collective-permute-done.4.refs_6_.refs_7_ = bf16[1,2,2,3584,256]{4,3,2,1,0:T(8,128)(2,1)} collective-permute-done((bf16[1,2,2,3584,256]{4,3,2,1,0:T(8,128)(2,1)}, bf16[1,2,2,3584,256]{4,3,2,1,0:T(8,128)(2,1)}, u32[]{:S(2)}, u32[]{:S(2)}) %collective-permute-start.4) | collective-permute-done | bytes 7340064 | tf_op jit(solution)/shard_map/ppermute | solution.py:25
  14.9 10.5 %collective-permute-done.refs_1_ = bf16[64,3712]{1,0:T(8,128)(2,1)S(1)} collective-permute-done((bf16[64,3712]{1,0:T(8,128)(2,1)}, bf16[64,3712]{1,0:T(8,128)(2,1)S(1)}, u32[]{:S(2)}, u32[]{:S(2)}) %collective-permute-start) | collective-permute-done | bytes 475168 | tf_op jit(solution)/shard_map/ppermute | solution.py:25
  28.4 2.7 %shard_map.88 = (bf16[80,3584]{1,0:T(8,128)(2,1)}, bf16[80,3584]{1,0:T(8,128)(2,1)}) custom-call(bf16[40,3584]{1,0:T(8,128)(2,1)} %get-tuple-element.54.refs_0_, bf16[40,3584]{1,0:T(8,128)(2,1)} %copy-done.12, bf16[40,3584]{1,0:T(8,128)(2,1)} %copy-done.14, bf16[40,3584]{1,0:T(8,128)(2,1)} %copy-done.13), custom_call_target="tpu_custom_call" | custom-call | flops 1000 | bytes 1000 | tf_op jit(solution)/shard_map/pallas_call | solution.py:231
  33.1 11.5 %collective-permute-done.2.refs_3_ = bf16[64,3712]{1,0:T(8,128)(2,1)S(1)} collective-permute-done((bf16[64,3712]{1,0:T(8,128)(2,1)}, bf16[64,3712]{1,0:T(8,128)(2,1)S(1)}, u32[]{:S(2)}, u32[]{:S(2)}) %collective-permute-start.2) | collective-permute-done | bytes 475168 | tf_op jit(solution)/shard_map/ppermute | solution.py:25
  46.5 5.2 %shard_map.89 = (bf16[80,3584]{1,0:T(8,128)(2,1)}, bf16[80,3584]{1,0:T(8,128)(2,1)}, bf16[80,3584]{1,0:T(8,128)(2,1)}, bf16[80,3584]{1,0:T(8,128)(2,1)}, bf16[32...) custom-call(bf16[64,3712]{1,0:T(8,128)(2,1)} %shard_map.86.refs_0_, bf16[64,3712]{1,0:T(8,128)(2,1)} %copy-done.7, ...), custom_call_target="tpu_custom_call" | custom-call | flops 1000 | bytes 1000 | tf_op jit(solution)/shard_map/pallas_call | solution.py:197
  55.6 15.8 %collective-permute-done.17.refs_1_ = bf16[80,3584]{1,0:T(8,128)(2,1)} collective-permute-done((bf16[80,3584]{1,0:T(8,128)(2,1)}, bf16[80,3584]{1,0:T(8,128)(2,1)}, u32[]{:S(2)}, u32[]{:S(2)}) %collective-permute-start.17) | collective-permute-done | bytes 573472 | tf_op jit(solution)/shard_map/ppermute | solution.py:25
  71.5 2.7 %collective-permute-start.19 = (bf16[80,3584]{1,0:T(8,128)(2,1)}, bf16[80,3584]{1,0:T(8,128)(2,1)}, u32[]{:S(2)}, u32[]{:S(2)}) collective-permute-start(bf16[80,3584]{1,0:T(8,128)(2,1)} %collective-permute-done.17.refs_1_), channel_id=1, source_target_pairs={{0,2},{1,3},{2,0},{3,1},{4,6},{5,7},{6,4},{7,5},{8,10},{9,11},{10,... | collective-permute-start | bytes 1720328 | tf_op jit(solution)/shard_map/ppermute | solution.py:25
  74.2 6.4 %collective-permute-done.10.refs_3_ = bf16[80,3584]{1,0:T(8,128)(2,1)} collective-permute-done((bf16[80,3584]{1,0:T(8,128)(2,1)}, bf16[80,3584]{1,0:T(8,128)(2,1)}, u32[]{:S(2)}, u32[]{:S(2)}) %collective-permute-start.10) | collective-permute-done | bytes 573472 | tf_op jit(solution)/shard_map/ppermute | solution.py:25
  80.5 9.4 %shard_map.90 = (bf16[80,3584]{1,0:T(8,128)(2,1)}, bf16[80,3584]{1,0:T(8,128)(2,1)}, bf16[80,3584]{1,0:T(8,128)(2,1)}, bf16[80,3584]{1,0:T(8,128)(2,1)}) custom-call(bf16[80,3584]{1,0:T(8,128)(2,1)} %get-tuple-element.64.refs_0_, bf16[80,3584]{1,0:T(8,128)(2,1)} %collective-permute-done.8.refs_1_, bf16[80,3584]{1,0:T(8,128)(2,1)} %collective-permute-done.9.refs_2_, ...), custom_call_target="tpu_custom_call" | custom-call | flops 1000 | bytes 1000 | tf_op jit(solution)/shard_map/pallas_call | solution.py:309
  90.0 2.3 %collective-permute-start.12 = (bf16[80,3584]{1,0:T(8,128)(2,1)}, bf16[80,3584]{1,0:T(8,128)(2,1)S(1)}, u32[]{:S(2)}, u32[]{:S(2)}) collective-permute-start(bf16[80,3584]{1,0:T(8,128)(2,1)} %get-tuple-element.70), channel_id=1, source_target_pairs={{0,16},{1,17},{2,18},{3,19},{4,20},{5,21},{6,22},{7,23},{8,24},{9,... | collective-permute-start | bytes 1720328 | tf_op jit(solution)/shard_map/ppermute | solution.py:25
  94.3 9.4 %shard_map.92 = (bf16[80,3584]{1,0:T(8,128)(2,1)}, bf16[80,3584]{1,0:T(8,128)(2,1)}, bf16[80,3584]{1,0:T(8,128)(2,1)}, bf16[80,3584]{1,0:T(8,128)(2,1)}) custom-call(bf16[80,3584]{1,0:T(8,128)(2,1)} %get-tuple-element.79.refs_0_, bf16[80,3584]{1,0:T(8,128)(2,1)} %collective-permute-done.17.refs_1_, bf16[80,3584]{1,0:T(8,128)(2,1)} %collective-permute-done.18.refs_2_, ...), custom_call_target="tpu_custom_call" | custom-call | flops 1000 | bytes 1000 | tf_op jit(solution)/shard_map/pallas_call | solution.py:309
  105.3 11.3 %collective-permute-done.12.refs_2_ = bf16[80,3584]{1,0:T(8,128)(2,1)S(1)} collective-permute-done((bf16[80,3584]{1,0:T(8,128)(2,1)}, bf16[80,3584]{1,0:T(8,128)(2,1)S(1)}, u32[]{:S(2)}, u32[]{:S(2)}) %collective-permute-start.12) | collective-permute-done | bytes 573472 | tf_op jit(solution)/shard_map/ppermute | solution.py:25
  119.1 5.1 %shard_map.91 = (f32[64,1792]{1,0:T(8,128)}, f32[64,1792]{1,0:T(8,128)}, f32[64,1792]{1,0:T(8,128)}, f32[64,1792]{1,0:T(8,128)}, bf16[64,3584]{1,0:T(8,128)(2,1)}, /*index=5*/bf16[64,3584]{1,0:T(8,128)(2,1)}) custom-call(bf16[320,256]{1,0:T(8,128)(2,1)} %get-tuple-element.62.high_ref, bf16[320,256]{1,0:T(8,128)(2,1)} %get-tuple-element.63.low_ref, ...), custom_call_target="tpu_custom_call" | custom-call | flops 1000 | bytes 1000 | tf_op jit(solution)/shard_map/pallas_call | solution.py:364
  125.3 4.2 %collective-permute-done.21 = bf16[80,3584]{1,0:T(8,128)(2,1)S(1)} collective-permute-done((bf16[80,3584]{1,0:T(8,128)(2,1)}, bf16[80,3584]{1,0:T(8,128)(2,1)S(1)}, u32[]{:S(2)}, u32[]{:S(2)}) %collective-permute-start.21) | collective-permute-done | bytes 573472 | tf_op jit(solution)/shard_map/ppermute | solution.py:25
  132.6 13.0 %collective-permute-done.15 = bf16[64,3584]{1,0:T(8,128)(2,1)S(1)} collective-permute-done((bf16[64,3584]{1,0:T(8,128)(2,1)}, bf16[64,3584]{1,0:T(8,128)(2,1)S(1)}, u32[]{:S(2)}, u32[]{:S(2)}) %collective-permute-start.15) | collective-permute-done | bytes 458784 | tf_op jit(solution)/shard_map/ppermute | solution.py:25
  147.7 2.5 %collective-permute-start.16 = (bf16[64,1792]{1,0:T(8,128)(2,1)}, bf16[64,1792]{1,0:T(8,128)(2,1)}, u32[]{:S(2)}, u32[]{:S(2)}) collective-permute-start(bf16[64,1792]{1,0:T(8,128)(2,1)} %get-tuple-element.101), channel_id=1, source_target_pairs={{0,4},{1,5},{2,6},{3,7},{4,0},{5,1},{6,2},{7,3},{8,12},{9,13},{10,... | collective-permute-start | bytes 688136 | tf_op jit(solution)/shard_map/ppermute | solution.py:25
  152.9 2.9 %shard_map.93 = (bf16[40,3584]{1,0:T(8,128)(2,1)}, bf16[40,3584]{1,0:T(8,128)(2,1)}, bf16[40,3584]{1,0:T(8,128)(2,1)}, bf16[40,3584]{1,0:T(8,128)(2,1)}) custom-call(bf16[80,3584]{1,0:T(8,128)(2,1)} %get-tuple-element.82.near_ref, bf16[80,3584]{1,0:T(8,128)(2,1)} %copy-done.5, bf16[80,3584]{1,0:T(8,128)(2,1)} %copy-done.6), custom_call_target="tpu_custom_call" | custom-call | flops 1000 | bytes 1000 | tf_op jit(solution)/shard_map/pallas_call | solution.py:252
  157.7 9.3 %collective-permute-done.16 = bf16[64,1792]{1,0:T(8,128)(2,1)} collective-permute-done((bf16[64,1792]{1,0:T(8,128)(2,1)}, bf16[64,1792]{1,0:T(8,128)(2,1)}, u32[]{:S(2)}, u32[]{:S(2)}) %collective-permute-start.16) | collective-permute-done | bytes 229408 | tf_op jit(solution)/shard_map/ppermute | solution.py:25
  168.0 4.9 %collective-permute-start.28 = (bf16[64,1792]{1,0:T(8,128)(2,1)S(1)}, bf16[64,1792]{1,0:T(8,128)(2,1)S(1)}, u32[]{:S(2)}, u32[]{:S(2)}) collective-permute-start(bf16[64,1792]{1,0:T(8,128)(2,1)S(1)} %fusion.3), channel_id=1, source_target_pairs={{32,0},{64,32},{96,64},{128,96},{160,128},{192,160},{224,192},{33,... | collective-permute-start | bytes 688136 | tf_op jit(solution)/shard_map/ppermute | solution.py:43
  173.8 2.8 %shard_map.94 = bf16[64,3584]{1,0:T(8,128)(2,1)} custom-call(bf16[192,64]{1,0:T(8,128)(2,1)} %get-tuple-element.92.high_ref, bf16[192,64]{1,0:T(8,128)(2,1)} %get-tuple-element.93.low_ref, bf16[40,3584]{1,0:T(8,128)(2,1)} %get-tuple-element.94.refs_0_, bf16[40,3584]{1,0:T(8,128)(2,1)} %copy-done.15, bf16[40,3584]{1,0:T(8,128)(2,1)} %copy-done.16, ...), custom_call_target="tpu_custom_call" | custom-call | flops 1000 | bytes 1000 | tf_op jit(solution)/shard_map/pallas_call | solution.py:338
  178.7 9.4 %collective-permute-start.29 = (bf16[64,1792]{1,0:T(8,128)(2,1)S(1)}, bf16[64,1792]{1,0:T(8,128)(2,1)S(1)}, u32[]{:S(2)}, u32[]{:S(2)}) collective-permute-start(bf16[64,1792]{1,0:T(8,128)(2,1)S(1)} %fusion.2), channel_id=1, source_target_pairs={{32,0},{64,32},{96,64},{128,96},{160,128},{192,160},{224,192},{33,... | collective-permute-start | bytes 688136 | tf_op jit(solution)/shard_map/ppermute | solution.py:43
  188.1 16.8 %collective-permute-done.27 = bf16[64,3584]{1,0:T(8,128)(2,1)S(1)} collective-permute-done((bf16[64,3584]{1,0:T(8,128)(2,1)}, bf16[64,3584]{1,0:T(8,128)(2,1)S(1)}, u32[]{:S(2)}, u32[]{:S(2)}) %collective-permute-start.27) | collective-permute-done | bytes 458784 | tf_op jit(solution)/shard_map/ppermute | solution.py:43
  (87 shorter events, 39.6 us)
Async XLA Ops:
  3.4 22.0 %collective-permute-start = (bf16[64,3712]{1,0:T(8,128)(2,1)}, bf16[64,3712]{1,0:T(8,128)(2,1)S(1)}, u32[]{:S(2)}, u32[]{:S(2)}) collective-permute-start(bf16[64,3712]{1,0:T(8,128)(2,1)} %shard_map.86.refs_0_), channel_id=1, source_target_pairs={{0,4},{1,5},{2,6},{3,7},{4,0},{5,1},{6,2},{7,3},{8,12},{9,13},{10,... | collective-permute-start | bytes 1425416 | tf_op jit(solution)/shard_map/ppermute | solution.py:25
  4.6 22.2 %collective-permute-start.1 = (bf16[64,3712]{1,0:T(8,128)(2,1)}, bf16[64,3712]{1,0:T(8,128)(2,1)S(1)}, u32[]{:S(2)}, u32[]{:S(2)}) collective-permute-start(bf16[64,3712]{1,0:T(8,128)(2,1)} %shard_map.86.refs_0_), channel_id=1, source_target_pairs={{0,2},{1,3},{2,0},{3,1},{4,6},{5,7},{6,4},{7,5},{8,10},{9,11},{10,... | collective-permute-start | bytes 1425416 | tf_op jit(solution)/shard_map/ppermute | solution.py:25
  8.1 18.8 %collective-permute-start.3 = (bf16[40,3584]{1,0:T(8,128)(2,1)}, bf16[40,3584]{1,0:T(8,128)(2,1)S(1)}, u32[]{:S(2)}, u32[]{:S(2)}) collective-permute-start(bf16[40,3584]{1,0:T(8,128)(2,1)} %get-tuple-element.55), channel_id=1, source_target_pairs={{0,8},{1,9},{2,10},{3,11},{4,12},{5,13},{6,14},{7,15},{8,16},{9,17... | collective-permute-start | bytes 860168 | tf_op jit(solution)/shard_map/ppermute | solution.py:25
  9.3 17.6 %collective-permute-start.6 = (bf16[40,3584]{1,0:T(8,128)(2,1)}, bf16[40,3584]{1,0:T(8,128)(2,1)S(1)}, u32[]{:S(2)}, u32[]{:S(2)}) collective-permute-start(bf16[40,3584]{1,0:T(8,128)(2,1)} %get-tuple-element.58), channel_id=1, source_target_pairs={{0,24},{1,25},{2,26},{3,27},{4,28},{5,29},{6,30},{7,31},{8,0},{9,1... | collective-permute-start | bytes 860168 | tf_op jit(solution)/shard_map/ppermute | solution.py:25
  44.6 26.9 %collective-permute-start.17 = (bf16[80,3584]{1,0:T(8,128)(2,1)}, bf16[80,3584]{1,0:T(8,128)(2,1)}, u32[]{:S(2)}, u32[]{:S(2)}) collective-permute-start(bf16[80,3584]{1,0:T(8,128)(2,1)} %get-tuple-element.78), channel_id=1, source_target_pairs={{0,4},{1,5},{2,6},{3,7},{4,0},{5,1},{6,2},{7,3},{8,12},{9,13},{10,... | collective-permute-start | bytes 1720328 | tf_op jit(solution)/shard_map/ppermute | solution.py:25
  46.2 25.3 %collective-permute-start.18 = (bf16[80,3584]{1,0:T(8,128)(2,1)}, bf16[80,3584]{1,0:T(8,128)(2,1)}, u32[]{:S(2)}, u32[]{:S(2)}) collective-permute-start(bf16[80,3584]{1,0:T(8,128)(2,1)} %get-tuple-element.79.refs_0_), channel_id=1, source_target_pairs={{0,2},{1,3},{2,0},{3,1},{4,6},{5,7},{6,4},{7,5},{8,10},{9,11},{10,... | collective-permute-start | bytes 1720328 | tf_op jit(solution)/shard_map/ppermute | solution.py:25
  51.7 22.4 %collective-permute-start.8 = (bf16[80,3584]{1,0:T(8,128)(2,1)}, bf16[80,3584]{1,0:T(8,128)(2,1)}, u32[]{:S(2)}, u32[]{:S(2)}) collective-permute-start(bf16[80,3584]{1,0:T(8,128)(2,1)} %get-tuple-element.65), channel_id=1, source_target_pairs={{0,8},{1,9},{2,10},{3,11},{4,12},{5,13},{6,14},{7,15},{8,16},{9,17... | collective-permute-start | bytes 1720328 | tf_op jit(solution)/shard_map/ppermute | solution.py:25
  52.9 21.2 %collective-permute-start.9 = (bf16[80,3584]{1,0:T(8,128)(2,1)}, bf16[80,3584]{1,0:T(8,128)(2,1)}, u32[]{:S(2)}, u32[]{:S(2)}) collective-permute-start(bf16[80,3584]{1,0:T(8,128)(2,1)} %get-tuple-element.66), channel_id=1, source_target_pairs={{0,16},{1,17},{2,18},{3,19},{4,20},{5,21},{6,22},{7,23},{8,24},{9,... | collective-permute-start | bytes 1720328 | tf_op jit(solution)/shard_map/ppermute | solution.py:25
  53.8 26.8 %collective-permute-start.10 = (bf16[80,3584]{1,0:T(8,128)(2,1)}, bf16[80,3584]{1,0:T(8,128)(2,1)}, u32[]{:S(2)}, u32[]{:S(2)}) collective-permute-start(bf16[80,3584]{1,0:T(8,128)(2,1)} %get-tuple-element.67), channel_id=1, source_target_pairs={{0,24},{1,25},{2,26},{3,27},{4,28},{5,29},{6,30},{7,31},{8,0},{9,1... | collective-permute-start | bytes 1720328 | tf_op jit(solution)/shard_map/ppermute | solution.py:25
  71.5 22.8 %collective-permute-start.19 = (bf16[80,3584]{1,0:T(8,128)(2,1)}, bf16[80,3584]{1,0:T(8,128)(2,1)}, u32[]{:S(2)}, u32[]{:S(2)}) collective-permute-start(bf16[80,3584]{1,0:T(8,128)(2,1)} %collective-permute-done.17.refs_1_), channel_id=1, source_target_pairs={{0,2},{1,3},{2,0},{3,1},{4,6},{5,7},{6,4},{7,5},{8,10},{9,11},{10,... | collective-permute-start | bytes 1720328 | tf_op jit(solution)/shard_map/ppermute | solution.py:25
  90.0 26.6 %collective-permute-start.12 = (bf16[80,3584]{1,0:T(8,128)(2,1)}, bf16[80,3584]{1,0:T(8,128)(2,1)S(1)}, u32[]{:S(2)}, u32[]{:S(2)}) collective-permute-start(bf16[80,3584]{1,0:T(8,128)(2,1)} %get-tuple-element.70), channel_id=1, source_target_pairs={{0,16},{1,17},{2,18},{3,19},{4,20},{5,21},{6,22},{7,23},{8,24},{9,... | collective-permute-start | bytes 1720328 | tf_op jit(solution)/shard_map/ppermute | solution.py:25
  92.3 25.9 %collective-permute-start.13 = (bf16[80,3584]{1,0:T(8,128)(2,1)}, bf16[80,3584]{1,0:T(8,128)(2,1)S(1)}, u32[]{:S(2)}, u32[]{:S(2)}) collective-permute-start(bf16[80,3584]{1,0:T(8,128)(2,1)} %get-tuple-element.71), channel_id=1, source_target_pairs={{0,8},{1,9},{2,10},{3,11},{4,12},{5,13},{6,14},{7,15},{8,16},{9,17... | collective-permute-start | bytes 1720328 | tf_op jit(solution)/shard_map/ppermute | solution.py:25
  103.7 21.5 %collective-permute-start.20 = (bf16[80,3584]{1,0:T(8,128)(2,1)}, bf16[80,3584]{1,0:T(8,128)(2,1)S(1)}, u32[]{:S(2)}, u32[]{:S(2)}) collective-permute-start(bf16[80,3584]{1,0:T(8,128)(2,1)} %get-tuple-element.83), channel_id=1, source_target_pairs={{0,2},{1,3},{2,0},{3,1},{4,6},{5,7},{6,4},{7,5},{8,10},{9,11},{10,... | collective-permute-start | bytes 1720328 | tf_op jit(solution)/shard_map/ppermute | solution.py:25
  105.0 24.5 %collective-permute-start.21 = (bf16[80,3584]{1,0:T(8,128)(2,1)}, bf16[80,3584]{1,0:T(8,128)(2,1)S(1)}, u32[]{:S(2)}, u32[]{:S(2)}) collective-permute-start(bf16[80,3584]{1,0:T(8,128)(2,1)} %get-tuple-element.85), channel_id=1, source_target_pairs={{0,2},{1,3},{2,0},{3,1},{4,6},{5,7},{6,4},{7,5},{8,10},{9,11},{10,... | collective-permute-start | bytes 1720328 | tf_op jit(solution)/shard_map/ppermute | solution.py:25
  124.1 21.5 %collective-permute-start.15 = (bf16[64,3584]{1,0:T(8,128)(2,1)}, bf16[64,3584]{1,0:T(8,128)(2,1)S(1)}, u32[]{:S(2)}, u32[]{:S(2)}) collective-permute-start(bf16[64,3584]{1,0:T(8,128)(2,1)} %get-tuple-element.75), channel_id=1, source_target_pairs={{0,2},{1,3},{2,0},{3,1},{4,6},{5,7},{6,4},{7,5},{8,10},{9,11},{10,... | collective-permute-start | bytes 1376264 | tf_op jit(solution)/shard_map/ppermute | solution.py:25
  130.7 21.4 %collective-permute-start.22 = (bf16[80,3584]{1,0:T(8,128)(2,1)S(1)}, bf16[80,3584]{1,0:T(8,128)(2,1)S(1)}, u32[]{:S(2)}, u32[]{:S(2)}) collective-permute-start(bf16[80,3584]{1,0:T(8,128)(2,1)S(1)} %add_convert_fusion), channel_id=1, source_target_pairs={{0,4},{1,5},{2,6},{3,7},{4,0},{5,1},{6,2},{7,3},{8,12},{9,13},{10,... | collective-permute-start | bytes 1720328 | tf_op jit(solution)/shard_map/ppermute | solution.py:25
  132.3 34.6 %collective-permute-start.14 = (bf16[64,3584]{1,0:T(8,128)(2,1)}, bf16[64,3584]{1,0:T(8,128)(2,1)S(1)}, u32[]{:S(2)}, u32[]{:S(2)}) collective-permute-start(bf16[64,3584]{1,0:T(8,128)(2,1)} %get-tuple-element.73), channel_id=1, source_target_pairs={{0,2},{1,3},{2,0},{3,1},{4,6},{5,7},{6,4},{7,5},{8,10},{9,11},{10,... | collective-permute-start | bytes 1376264 | tf_op jit(solution)/shard_map/ppermute | solution.py:25
  147.7 19.3 %collective-permute-start.16 = (bf16[64,1792]{1,0:T(8,128)(2,1)}, bf16[64,1792]{1,0:T(8,128)(2,1)}, u32[]{:S(2)}, u32[]{:S(2)}) collective-permute-start(bf16[64,1792]{1,0:T(8,128)(2,1)} %get-tuple-element.101), channel_id=1, source_target_pairs={{0,4},{1,5},{2,6},{3,7},{4,0},{5,1},{6,2},{7,3},{8,12},{9,13},{10,... | collective-permute-start | bytes 688136 | tf_op jit(solution)/shard_map/ppermute | solution.py:25
  155.8 17.2 %collective-permute-start.24 = (bf16[40,3584]{1,0:T(8,128)(2,1)}, bf16[40,3584]{1,0:T(8,128)(2,1)S(1)}, u32[]{:S(2)}, u32[]{:S(2)}) collective-permute-start(bf16[40,3584]{1,0:T(8,128)(2,1)} %get-tuple-element.95), channel_id=1, source_target_pairs={{0,24},{1,25},{2,26},{3,27},{4,28},{5,29},{6,30},{7,31},{8,0},{9,1... | collective-permute-start | bytes 860168 | tf_op jit(solution)/shard_map/ppermute | solution.py:25
  156.3 16.6 %collective-permute-start.25 = (bf16[40,3584]{1,0:T(8,128)(2,1)}, bf16[40,3584]{1,0:T(8,128)(2,1)S(1)}, u32[]{:S(2)}, u32[]{:S(2)}) collective-permute-start(bf16[40,3584]{1,0:T(8,128)(2,1)} %get-tuple-element.96), channel_id=1, source_target_pairs={{0,16},{1,17},{2,18},{3,19},{4,20},{5,21},{6,22},{7,23},{8,24},{9,... | collective-permute-start | bytes 860168 | tf_op jit(solution)/shard_map/ppermute | solution.py:25
  156.9 16.1 %collective-permute-start.26 = (bf16[40,3584]{1,0:T(8,128)(2,1)}, bf16[40,3584]{1,0:T(8,128)(2,1)S(1)}, u32[]{:S(2)}, u32[]{:S(2)}) collective-permute-start(bf16[40,3584]{1,0:T(8,128)(2,1)} %get-tuple-element.97), channel_id=1, source_target_pairs={{0,8},{1,9},{2,10},{3,11},{4,12},{5,13},{6,14},{7,15},{8,16},{9,17... | collective-permute-start | bytes 860168 | tf_op jit(solution)/shard_map/ppermute | solution.py:25
  168.0 37.8 %collective-permute-start.28 = (bf16[64,1792]{1,0:T(8,128)(2,1)S(1)}, bf16[64,1792]{1,0:T(8,128)(2,1)S(1)}, u32[]{:S(2)}, u32[]{:S(2)}) collective-permute-start(bf16[64,1792]{1,0:T(8,128)(2,1)S(1)} %fusion.3), channel_id=1, source_target_pairs={{32,0},{64,32},{96,64},{128,96},{160,128},{192,160},{224,192},{33,... | collective-permute-start | bytes 688136 | tf_op jit(solution)/shard_map/ppermute | solution.py:43
  176.7 28.2 %collective-permute-start.27 = (bf16[64,3584]{1,0:T(8,128)(2,1)}, bf16[64,3584]{1,0:T(8,128)(2,1)S(1)}, u32[]{:S(2)}, u32[]{:S(2)}) collective-permute-start(bf16[64,3584]{1,0:T(8,128)(2,1)} %shard_map.94), channel_id=1, source_target_pairs={{0,32},{32,64},{64,96},{96,128},{128,160},{160,192},{192,224},{1,3... | collective-permute-start | bytes 1376264 | tf_op jit(solution)/shard_map/ppermute | solution.py:43
  178.7 27.1 %collective-permute-start.29 = (bf16[64,1792]{1,0:T(8,128)(2,1)S(1)}, bf16[64,1792]{1,0:T(8,128)(2,1)S(1)}, u32[]{:S(2)}, u32[]{:S(2)}) collective-permute-start(bf16[64,1792]{1,0:T(8,128)(2,1)S(1)} %fusion.2), channel_id=1, source_target_pairs={{32,0},{64,32},{96,64},{128,96},{160,128},{192,160},{224,192},{33,... | collective-permute-start | bytes 688136 | tf_op jit(solution)/shard_map/ppermute | solution.py:43
  (24 other events, 313.4 us)

commit v2 on v1

--- a/solution.py
+++ b/solution.py
@@ -106,7 +106,7 @@
     ]
 
 
-def routes(facts, group, capacity, stride, hot_ref, high_ref, low_ref):
+def routes(facts, group, capacity, stride, hot_ref, weight_ref):
     tokens = facts[0].shape[1]
     count = group * X
     place = lax.axis_index("expert")
@@ -139,11 +139,9 @@
         slot = jnp.where(row < group * capacity, slot + 1, -1)
         here = wanted == slot.astype(jnp.float32)
         weight = jnp.where(here, weight, 0.0)
-        high = weight.astype(jnp.bfloat16)
         at = slice(k * stride, (k + 1) * stride)
         hot_ref[at] = jnp.where(here, 1.0, 0.0).astype(jnp.bfloat16)
-        high_ref[at] = high
-        low_ref[at] = (weight - high.astype(jnp.float32)).astype(jnp.bfloat16)
+        weight_ref[at] = weight.astype(jnp.bfloat16)
 
 
 def norm_line(values, gains, ids, gates, slot):
@@ -160,10 +158,10 @@
     _, rows, width = values.shape
 
     def kernel(x_ref, gain_ref, ids_ref, gates_ref, *refs):
-        outs, (high, low, hot, held) = refs[:X], refs[X:]
+        outs, (weights, hot, held) = refs[:X], refs[X:]
         facts = [ids_ref[0, slot, r : r + 1].astype(jnp.float32) for r in range(2)]
         facts += [gates_ref[0, slot, r : r + 1] for r in range(2)]
-        routes(facts, 2, CAP, STRIDE, hot, high, low)
+        routes(facts, 2, CAP, STRIDE, hot, weights)
         held[...] = normed_of(x_ref[0], gain_ref[0, slot : slot + 1])
         for at in pieces(width):
             value = dot(hot[...], held[:, at]).astype(jnp.bfloat16)
@@ -172,7 +170,7 @@
 
     return call(
         kernel,
-        [shaped(2 * CAP, width)] * X + [shaped(X * STRIDE, rows)] * 2,
+        [shaped(2 * CAP, width)] * X + [shaped(X * STRIDE, rows)],
         scratch_shapes=[
             pltpu.VMEM((X * STRIDE, rows), jnp.bfloat16),
             pltpu.VMEM((rows, width), jnp.bfloat16),
@@ -185,10 +183,10 @@
     tokens, slots = Z * rows, Z * CAP
 
     def kernel(*refs):
-        ins, outs, (high, low, hot, held) = refs[:Z], refs[Z : Z + X], refs[Z + X :]
+        ins, outs, (weights, hot, held) = refs[:Z], refs[Z : Z + X], refs[Z + X :]
         for n in range(Z):
             held[n * rows : (n + 1) * rows] = ins[n][...]
-        routes(unpacked(held[:, width:]), 1, slots, slots, hot, high, low)
+        routes(unpacked(held[:, width:]), 1, slots, slots, hot, weights)
         for at in pieces(width):
             value = dot(hot[...], held[:, at]).astype(jnp.bfloat16)
             for k in range(X):
@@ -196,7 +194,7 @@
 
     return call(
         kernel,
-        [shaped(slots, width)] * X + [shaped(X * slots, tokens)] * 2,
+        [shaped(slots, width)] * X + [shaped(X * slots, tokens)],
         scratch_shapes=[
             pltpu.VMEM((X * slots, tokens), jnp.bfloat16),
             pltpu.VMEM((tokens, width + FACTS), jnp.bfloat16),
@@ -321,41 +319,39 @@
     )(*blocks, own, own, peer, peer, own_down, peer_down)
 
 
-def combine_own(high, low, blocks, values):
+def combine_own(weights, blocks, values):
     slots, width = blocks[0].shape
-    tokens = high.shape[1]
-
-    def kernel(high_ref, low_ref, *refs):
+    tokens = weights.shape[1]
+
+    def kernel(weight_ref, *refs):
         ins, x_ref, out, held = refs[:X], refs[X], refs[X + 1], refs[X + 2]
         held[...] = jnp.zeros_like(held)
         for k in range(X):
             held[k * STRIDE : k * STRIDE + slots] = ins[k][...]
         for at in pieces(width):
-            mixture = dot(high_ref[...], held[:, at], ((0,), (0,)))
-            mixture += dot(low_ref[...], held[:, at], ((0,), (0,)))
+            mixture = dot(weight_ref[...], held[:, at], ((0,), (0,)))
             out[:, at] = (x_ref[0, :, at].astype(jnp.float32) + mixture).astype(jnp.bfloat16)
 
     return call(
         kernel,
         shaped(tokens, width),
         scratch_shapes=[pltpu.VMEM((X * STRIDE, width), jnp.bfloat16)],
-    )(high, low, *blocks, values)
-
-
-def combine_line(high, low, blocks):
+    )(weights, *blocks, values)
+
+
+def combine_line(weights, blocks):
     slots, width = blocks[0].shape
-    tokens = high.shape[1]
+    tokens = weights.shape[1]
     rows, part = tokens // Z, width // HALVES
 
-    def kernel(high_ref, low_ref, *refs):
+    def kernel(weight_ref, *refs):
         ins, keep, send, held = refs[:X], refs[X : X + 2 * HALVES], refs[-3:-1], refs[-1]
         for k in range(X):
             held[k * slots : (k + 1) * slots] = ins[k][...]
         for h in range(HALVES):
             for at in pieces(part):
                 there = slice(h * part + at.start, h * part + at.stop)
-                total = dot(high_ref[...], held[:, there], ((0,), (0,)))
-                total += dot(low_ref[...], held[:, there], ((0,), (0,)))
+                total = dot(weight_ref[...], held[:, there], ((0,), (0,)))
                 for n in range(2):
                     keep[2 * h + n][:, at] = total[n * rows : (n + 1) * rows]
                     lower = slice((2 + n) * rows, (3 + n) * rows)
@@ -365,7 +361,7 @@
         kernel,
         [shaped(rows, part, kind=jnp.float32)] * (2 * HALVES) + [shaped(rows, width)] * 2,
         scratch_shapes=[pltpu.VMEM((X * slots, width), jnp.bfloat16)],
-    )(high, low, *blocks)
+    )(weights, *blocks)
     return keep[::2], keep[1::2], side, corner
 
 
@@ -375,18 +371,18 @@
     normed = norm_line(falling, norm_gains, ids, gates, 1)
     side, far = across_z(normed, 1), across_z(normed, 2)
     peer_up = across_cores(gate_up)
-    *own, own_high, own_low = dispatch_own(rising, after(norm_gains, normed), ids, gates, 0)
+    *own, own_weights = dispatch_own(rising, after(norm_gains, normed), ids, gates, 0)
     own[2] = after(own[2], peer_up)
     own = [own[0]] + [along_x(own[k], k) for k in range(1, X)]
     far = after(far, own[0])
     corner = across_z(far, 1)
-    own[0] = after(own[0], far, side)
+    peer_down = across_cores(after(down_proj, far, side, *own[1:]))
+    own[0] = after(own[0], peer_down)
     near0, far0 = by_half(own)
-    peer_down = across_cores(after(down_proj, near0))
     far0 = across_z(after(far0, corner), 2)
     side0 = across_z(after(near0, corner), 1)
 
-    *line, line_high, line_low = dispatch_line([normed, far, side, after(corner, peer_down)])
+    *line, line_weights = dispatch_line([normed, far, side, after(corner, peer_down)])
     far0 = after(far0, line[0], side0)
     rows0 = [near0, far0, side0, across_z(far0, 1)]
     rows1 = [line[0]] + [along_x(line[k], k) for k in range(1, X)]
@@ -396,16 +392,17 @@
     line = [line[0]] + [along_x(line[k], -k) for k in range(1, X)]
     near0, far0, side0, corner0 = experts(rows0, gate_up, down_proj, peer_up, peer_down, 0)
     corner0, side0 = across_z(corner0, 1), across_z(side0, 1)
-    near1, far1, side1, corner1 = combine_line(line_high, line_low, line)
-    far0 = across_z(plus(far0, after(corner0, near1[0], side0)), 2)
-    corner1, side1 = across_z(corner1, 1), across_z(side1, 1)
+    near1, far1, side1, corner1 = combine_line(line_weights, line)
+    far0 = plus(far0, after(corner0, near1[0], side0))
+    corner1, side1 = across_z(corner1, 1), across_z(after(side1, far0), 1)
+    far0 = across_z(far0, 2)
     width = falling.shape[2] // HALVES
     part = [slice(h * width, (h + 1) * width) for h in range(HALVES)]
     sent1 = [plus(far1[h], corner1[:, part[h]]) for h in range(HALVES)]
     own = by_column(after(near0, sent1[0]), side0, far0)
     own = [own[0]] + [along_x(own[k], -k) for k in range(1, X)]
     far1 = [across_z(sent1[0], 2)]
-    far1[0] = after(far1[0], own[0])
+    far1[0] = after(far1[0], own[1])
 
     def ended(h):
         mixture = near1[h] + (side1[:, part[h]].astype(jnp.float32) + far1[h].astype(jnp.float32))
@@ -415,7 +412,7 @@
     out1 = [ended(0)]
     got1 = [shifted(out1[0], -1)]
     own[0] = after(own[0], out1[0])
-    out0 = combine_own(own_high, own_low, own, rising)
+    out0 = combine_own(own_weights, own, rising)
     got0 = shifted(out0, 1)
     far1[1] = after(far1[1], out0)
     out1.append(ended(1))

time: 210 us -> 210 us (level); the launches traced: 207 us -> 210 us
  starting transfers between devices: 46.2 us -> 52.3 us
    ppermute x3, starting transfers between devices: 16.2 us -> 22.1 us  [shifted(): return lax.ppermute(block, 'section', route)]
  transfers between devices with their start and end apart: 30 -> 30, of which waited for: 13 -> 15; matrix products, arithmetic and copies ran while one was open for 3% -> 2% of each run, Pallas kernels for 19% -> 19%
where the time goes in v2:
time: 210 us
  waiting for transfers between devices  109 us (52%)
  starting transfers between devices  52.3 us (25%)
  Pallas kernels  40.4 us (19%)
  other arithmetic  4.59 us (2%)
  local copies, waits for them, and re-layouts  3.25 us (2%)
    ppermute x27, waiting for transfers between devices, moved(): return lax.ppermute(block, 'expert', route)  89.9 us
    ppermute x27, starting transfers between devices, moved(): return lax.ppermute(block, 'expert', route)  30.2 us
    ppermute x3, starting transfers between devices, shifted(): return lax.ppermute(block, 'section', route)  22.1 us
    pallas_call x2, Pallas kernels, experts(): call(kernel, [shaped(slots, width)] * X, grid=(steps + down_steps,), in_s...  18.8 us
    ppermute x3, waiting for transfers between devices, shifted(): return lax.ppermute(block, 'section', route)  18.7 us
  transfers between devices with their start and end apart: 30, of which 15 were waited for; matrix products, arithmetic and copies ran while one was open for 2% of the time, Pallas kernels for 19%

profile of v2, /device:TPU:195, one launch (start us, length us, event | category | flops | bytes accessed | tf_op | source)
XLA Modules:
  0.0 210.0 jit_solution(17377677505569306790)
XLA Ops:
  5.3 2.7 %shard_map.87 = (bf16[40,3584]{1,0:T(8,128)(2,1)}, bf16[40,3584]{1,0:T(8,128)(2,1)}, bf16[40,3584]{1,0:T(8,128)(2,1)}, bf16[40,3584]{1,0:T(8,128)(2,1)}, bf16[192,64]{1,0:T(8,128)(2,1)}) custom-call(bf16[1,64,3584]{2,1,0:T(8,128)(2,1)} %refs_4_.5, f32[1,2,3584]{2,1,0:T(2,128)} %gain_ref.2, s32[1,2,2,64]{3,2,1,0:T(2,128)} %bitcast.13, f32[1,2,2,64]{3,2,1,0:T(2,128)} %bitcast.15), custom_call_target="tpu_custom_call" | custom-call | flops 1000 | bytes 1000 | tf_op jit(solution)/shard_map/pallas_call | solution.py:171
  9.5 3.5 %collective-permute-done.4.refs_6_.refs_7_ = bf16[1,2,2,3584,256]{4,3,2,1,0:T(8,128)(2,1)} collective-permute-done((bf16[1,2,2,3584,256]{4,3,2,1,0:T(8,128)(2,1)}, bf16[1,2,2,3584,256]{4,3,2,1,0:T(8,128)(2,1)}, u32[]{:S(2)}, u32[]{:S(2)}) %collective-permute-start.4) | collective-permute-done | bytes 7340064 | tf_op jit(solution)/shard_map/ppermute | solution.py:25
  14.9 10.5 %collective-permute-done.refs_1_ = bf16[64,3712]{1,0:T(8,128)(2,1)S(1)} collective-permute-done((bf16[64,3712]{1,0:T(8,128)(2,1)}, bf16[64,3712]{1,0:T(8,128)(2,1)S(1)}, u32[]{:S(2)}, u32[]{:S(2)}) %collective-permute-start) | collective-permute-done | bytes 475168 | tf_op jit(solution)/shard_map/ppermute | solution.py:25
  30.4 4.2 %collective-permute-done.7.refs_9_ = bf16[1,2,256,3584]{3,2,1,0:T(8,128)(2,1)S(1)} collective-permute-done((bf16[1,2,256,3584]{3,2,1,0:T(8,128)(2,1)}, bf16[1,2,256,3584]{3,2,1,0:T(8,128)(2,1)S(1)}, u32[]{:S(2)}, u32[]{:S(2)}) %collective-permute-start.7) | collective-permute-done | bytes 3670048 | tf_op jit(solution)/shard_map/ppermute | solution.py:25
  34.6 3.5 %shard_map.91 = (bf16[80,3584]{1,0:T(8,128)(2,1)}, bf16[80,3584]{1,0:T(8,128)(2,1)}) custom-call(bf16[40,3584]{1,0:T(8,128)(2,1)} %get-tuple-element.70.refs_0_, bf16[40,3584]{1,0:T(8,128)(2,1)} %copy-done.11, bf16[40,3584]{1,0:T(8,128)(2,1)} %collective-permute-done.5.refs_2_, bf16[40,3584]{1,0:T(8,128)(2,1)} %copy-done.12), custom_call_target="tpu_custom_call" | custom-call | flops 1000 | bytes 1000 | tf_op jit(solution)/shard_map/pallas_call | solution.py:229
  38.2 3.8 %collective-permute-done.2.refs_3_ = bf16[64,3712]{1,0:T(8,128)(2,1)} collective-permute-done((bf16[64,3712]{1,0:T(8,128)(2,1)}, bf16[64,3712]{1,0:T(8,128)(2,1)}, u32[]{:S(2)}, u32[]{:S(2)}) %collective-permute-start.2) | collective-permute-done | bytes 475168 | tf_op jit(solution)/shard_map/ppermute | solution.py:25
  43.9 3.9 %shard_map.88 = (bf16[80,3584]{1,0:T(8,128)(2,1)}, bf16[80,3584]{1,0:T(8,128)(2,1)}, bf16[80,3584]{1,0:T(8,128)(2,1)}, bf16[80,3584]{1,0:T(8,128)(2,1)}, bf16[320,256]{1,0:T(8,128)(2,1)}) custom-call(bf16[64,3712]{1,0:T(8,128)(2,1)} %shard_map.86.refs_0_, bf16[64,3712]{1,0:T(8,128)(2,1)} %copy-done.7, bf16[64,3712]{1,0:T(8,128)(2,1)} %copy-done.8, ...), custom_call_target="tpu_custom_call" | custom-call | flops 1000 | bytes 1000 | tf_op jit(solution)/shard_map/pallas_call | solution.py:195
  51.7 15.0 %collective-permute-done.15.refs_2_ = bf16[80,3584]{1,0:T(8,128)(2,1)} collective-permute-done((bf16[80,3584]{1,0:T(8,128)(2,1)}, bf16[80,3584]{1,0:T(8,128)(2,1)}, u32[]{:S(2)}, u32[]{:S(2)}) %collective-permute-start.15) | collective-permute-done | bytes 573472 | tf_op jit(solution)/shard_map/ppermute | solution.py:25
  69.0 7.5 %collective-permute-done.10.refs_3_ = bf16[80,3584]{1,0:T(8,128)(2,1)} collective-permute-done((bf16[80,3584]{1,0:T(8,128)(2,1)}, bf16[80,3584]{1,0:T(8,128)(2,1)}, u32[]{:S(2)}, u32[]{:S(2)}) %collective-permute-start.10) | collective-permute-done | bytes 573472 | tf_op jit(solution)/shard_map/ppermute | solution.py:25
  76.6 9.4 %shard_map.89 = (bf16[80,3584]{1,0:T(8,128)(2,1)}, bf16[80,3584]{1,0:T(8,128)(2,1)}, bf16[80,3584]{1,0:T(8,128)(2,1)}, bf16[80,3584]{1,0:T(8,128)(2,1)}) custom-call(bf16[80,3584]{1,0:T(8,128)(2,1)} %get-tuple-element.60.refs_0_, bf16[80,3584]{1,0:T(8,128)(2,1)} %collective-permute-done.8.refs_1_, bf16[80,3584]{1,0:T(8,128)(2,1)} %collective-permute-done.9.refs_2_, ...), custom_call_target="tpu_custom_call" | custom-call | flops 1000 | bytes 1000 | tf_op jit(solution)/shard_map/pallas_call | solution.py:307
  86.1 2.3 %collective-permute-start.12 = (bf16[80,3584]{1,0:T(8,128)(2,1)}, bf16[80,3584]{1,0:T(8,128)(2,1)S(1)}, u32[]{:S(2)}, u32[]{:S(2)}) collective-permute-start(bf16[80,3584]{1,0:T(8,128)(2,1)} %get-tuple-element.66), channel_id=1, source_target_pairs={{0,16},{1,17},{2,18},{3,19},{4,20},{5,21},{6,22},{7,23},{8,24},{9,... | collective-permute-start | bytes 1720328 | tf_op jit(solution)/shard_map/ppermute | solution.py:25
  90.4 9.4 %shard_map.92 = (bf16[80,3584]{1,0:T(8,128)(2,1)}, bf16[80,3584]{1,0:T(8,128)(2,1)}, bf16[80,3584]{1,0:T(8,128)(2,1)}, bf16[80,3584]{1,0:T(8,128)(2,1)}) custom-call(bf16[80,3584]{1,0:T(8,128)(2,1)} %get-tuple-element.75.refs_0_, bf16[80,3584]{1,0:T(8,128)(2,1)} %collective-permute-done.14.refs_1_, bf16[80,3584]{1,0:T(8,128)(2,1)} %collective-permute-done.15.refs_2_, ...), custom_call_target="tpu_custom_call" | custom-call | flops 1000 | bytes 1000 | tf_op jit(solution)/shard_map/pallas_call | solution.py:307
  101.3 11.3 %collective-permute-done.12.refs_2_ = bf16[80,3584]{1,0:T(8,128)(2,1)S(1)} collective-permute-done((bf16[80,3584]{1,0:T(8,128)(2,1)}, bf16[80,3584]{1,0:T(8,128)(2,1)S(1)}, u32[]{:S(2)}, u32[]{:S(2)}) %collective-permute-start.12) | collective-permute-done | bytes 573472 | tf_op jit(solution)/shard_map/ppermute | solution.py:25
  115.1 4.0 %shard_map.90 = (f32[64,1792]{1,0:T(8,128)}, f32[64,1792]{1,0:T(8,128)}, f32[64,1792]{1,0:T(8,128)}, f32[64,1792]{1,0:T(8,128)}, bf16[64,3584]{1,0:T(8,128)(2,1)}, /*index=5*/bf16[64,3584]{1,0:T(8,128)(2,1)}) custom-call(bf16[320,256]{1,0:T(8,128)(2,1)} %get-tuple-element.59.weight_ref, bf16[80,3584]{1,0:T(8,128)(2,1)} %get-tuple-element.64.refs_0_, ...), custom_call_target="tpu_custom_call" | custom-call | flops 1000 | bytes 1000 | tf_op jit(solution)/shard_map/pallas_call | solution.py:360
  120.4 5.0 %collective-permute-done.18.side_ref = bf16[80,3584]{1,0:T(8,128)(2,1)S(1)} collective-permute-done((bf16[80,3584]{1,0:T(8,128)(2,1)}, bf16[80,3584]{1,0:T(8,128)(2,1)S(1)}, u32[]{:S(2)}, u32[]{:S(2)}) %collective-permute-start.18) | collective-permute-done | bytes 573472 | tf_op jit(solution)/shard_map/ppermute | solution.py:25
  128.9 12.6 %collective-permute-done.20 = bf16[64,3584]{1,0:T(8,128)(2,1)S(1)} collective-permute-done((bf16[64,3584]{1,0:T(8,128)(2,1)}, bf16[64,3584]{1,0:T(8,128)(2,1)S(1)}, u32[]{:S(2)}, u32[]{:S(2)}) %collective-permute-start.20) | collective-permute-done | bytes 458784 | tf_op jit(solution)/shard_map/ppermute | solution.py:25
  142.7 5.4 %collective-permute-done.22.far_ref = bf16[80,3584]{1,0:T(8,128)(2,1)S(1)} collective-permute-done((bf16[80,3584]{1,0:T(8,128)(2,1)S(1)}, bf16[80,3584]{1,0:T(8,128)(2,1)S(1)}, u32[]{:S(2)}, u32[]{:S(2)}) %collective-permute-start.22) | collective-permute-done | bytes 573472 | tf_op jit(solution)/shard_map/ppermute | solution.py:25
  148.9 2.9 %shard_map.93 = (bf16[40,3584]{1,0:T(8,128)(2,1)}, bf16[40,3584]{1,0:T(8,128)(2,1)}, bf16[40,3584]{1,0:T(8,128)(2,1)}, bf16[40,3584]{1,0:T(8,128)(2,1)}) custom-call(bf16[80,3584]{1,0:T(8,128)(2,1)} %get-tuple-element.85.near_ref, bf16[80,3584]{1,0:T(8,128)(2,1)} %copy-done.5, bf16[80,3584]{1,0:T(8,128)(2,1)} %copy-done.6), custom_call_target="tpu_custom_call" | custom-call | flops 1000 | bytes 1000 | tf_op jit(solution)/shard_map/pallas_call | solution.py:250
  151.9 3.1 %collective-permute-start.21 = (bf16[64,1792]{1,0:T(8,128)(2,1)S(1)}, bf16[64,1792]{1,0:T(8,128)(2,1)S(1)}, u32[]{:S(2)}, u32[]{:S(2)}) collective-permute-start(bf16[64,1792]{1,0:T(8,128)(2,1)S(1)} %get-tuple-element.99), channel_id=1, source_target_pairs={{0,4},{1,5},{2,6},{3,7},{4,0},{5,1},{6,2},{7,3},{8,12},{9,13},{10,... | collective-permute-start | bytes 688136 | tf_op jit(solution)/shard_map/ppermute | solution.py:25
  156.5 5.5 %collective-permute-done.21 = bf16[64,1792]{1,0:T(8,128)(2,1)S(1)} collective-permute-done((bf16[64,1792]{1,0:T(8,128)(2,1)S(1)}, bf16[64,1792]{1,0:T(8,128)(2,1)S(1)}, u32[]{:S(2)}, u32[]{:S(2)}) %collective-permute-start.21) | collective-permute-done | bytes 229408 | tf_op jit(solution)/shard_map/ppermute | solution.py:25
  163.9 10.8 %collective-permute-start.28 = (bf16[64,1792]{1,0:T(8,128)(2,1)S(1)}, bf16[64,1792]{1,0:T(8,128)(2,1)S(1)}, u32[]{:S(2)}, u32[]{:S(2)}) collective-permute-start(bf16[64,1792]{1,0:T(8,128)(2,1)S(1)} %fusion.3), channel_id=1, source_target_pairs={{32,0},{64,32},{96,64},{128,96},{160,128},{192,160},{224,192},{33,... | collective-permute-start | bytes 688136 | tf_op jit(solution)/shard_map/ppermute | solution.py:43
  175.5 2.6 %shard_map.94 = bf16[64,3584]{1,0:T(8,128)(2,1)} custom-call(bf16[192,64]{1,0:T(8,128)(2,1)} %get-tuple-element.91.weight_ref, bf16[40,3584]{1,0:T(8,128)(2,1)} %get-tuple-element.93.refs_0_, bf16[40,3584]{1,0:T(8,128)(2,1)} %copy-done.13, bf16[40,3584]{1,0:T(8,128)(2,1)} %copy-done.14, bf16[40,3584]{1,0:T(8,128)(2,1)} %copy-done.15, ...), custom_call_target="tpu_custom_call" | custom-call | flops 1000 | bytes 1000 | tf_op jit(solution)/shard_map/pallas_call | solution.py:335
  180.1 9.4 %collective-permute-start.29 = (bf16[64,1792]{1,0:T(8,128)(2,1)S(1)}, bf16[64,1792]{1,0:T(8,128)(2,1)S(1)}, u32[]{:S(2)}, u32[]{:S(2)}) collective-permute-start(bf16[64,1792]{1,0:T(8,128)(2,1)S(1)} %fusion.2), channel_id=1, source_target_pairs={{32,0},{64,32},{96,64},{128,96},{160,128},{192,160},{224,192},{33,... | collective-permute-start | bytes 688136 | tf_op jit(solution)/shard_map/ppermute | solution.py:43
  189.5 18.7 %collective-permute-done.27 = bf16[64,3584]{1,0:T(8,128)(2,1)S(1)} collective-permute-done((bf16[64,3584]{1,0:T(8,128)(2,1)}, bf16[64,3584]{1,0:T(8,128)(2,1)S(1)}, u32[]{:S(2)}, u32[]{:S(2)}) %collective-permute-start.27) | collective-permute-done | bytes 458784 | tf_op jit(solution)/shard_map/ppermute | solution.py:43
  (83 shorter events, 42.1 us)
Async XLA Ops:
  3.4 22.0 %collective-permute-start = (bf16[64,3712]{1,0:T(8,128)(2,1)}, bf16[64,3712]{1,0:T(8,128)(2,1)S(1)}, u32[]{:S(2)}, u32[]{:S(2)}) collective-permute-start(bf16[64,3712]{1,0:T(8,128)(2,1)} %shard_map.86.refs_0_), channel_id=1, source_target_pairs={{0,4},{1,5},{2,6},{3,7},{4,0},{5,1},{6,2},{7,3},{8,12},{9,13},{10,... | collective-permute-start | bytes 1425416 | tf_op jit(solution)/shard_map/ppermute | solution.py:25
  4.6 22.2 %collective-permute-start.1 = (bf16[64,3712]{1,0:T(8,128)(2,1)}, bf16[64,3712]{1,0:T(8,128)(2,1)S(1)}, u32[]{:S(2)}, u32[]{:S(2)}) collective-permute-start(bf16[64,3712]{1,0:T(8,128)(2,1)} %shard_map.86.refs_0_), channel_id=1, source_target_pairs={{0,2},{1,3},{2,0},{3,1},{4,6},{5,7},{6,4},{7,5},{8,10},{9,11},{10,... | collective-permute-start | bytes 1425416 | tf_op jit(solution)/shard_map/ppermute | solution.py:25
  8.1 17.3 %collective-permute-start.3 = (bf16[40,3584]{1,0:T(8,128)(2,1)}, bf16[40,3584]{1,0:T(8,128)(2,1)S(1)}, u32[]{:S(2)}, u32[]{:S(2)}) collective-permute-start(bf16[40,3584]{1,0:T(8,128)(2,1)} %get-tuple-element.53), channel_id=1, source_target_pairs={{0,8},{1,9},{2,10},{3,11},{4,12},{5,13},{6,14},{7,15},{8,16},{9,17... | collective-permute-start | bytes 860168 | tf_op jit(solution)/shard_map/ppermute | solution.py:25
  9.3 16.1 %collective-permute-start.6 = (bf16[40,3584]{1,0:T(8,128)(2,1)}, bf16[40,3584]{1,0:T(8,128)(2,1)S(1)}, u32[]{:S(2)}, u32[]{:S(2)}) collective-permute-start(bf16[40,3584]{1,0:T(8,128)(2,1)} %get-tuple-element.56), channel_id=1, source_target_pairs={{0,24},{1,25},{2,26},{3,27},{4,28},{5,29},{6,30},{7,31},{8,0},{9,1... | collective-permute-start | bytes 860168 | tf_op jit(solution)/shard_map/ppermute | solution.py:25
  42.0 24.7 %collective-permute-start.15 = (bf16[80,3584]{1,0:T(8,128)(2,1)}, bf16[80,3584]{1,0:T(8,128)(2,1)}, u32[]{:S(2)}, u32[]{:S(2)}) collective-permute-start(bf16[80,3584]{1,0:T(8,128)(2,1)} %get-tuple-element.75.refs_0_), channel_id=1, source_target_pairs={{0,2},{1,3},{2,0},{3,1},{4,6},{5,7},{6,4},{7,5},{8,10},{9,11},{10,... | collective-permute-start | bytes 1720328 | tf_op jit(solution)/shard_map/ppermute | solution.py:25
  43.2 25.8 %collective-permute-start.14 = (bf16[80,3584]{1,0:T(8,128)(2,1)}, bf16[80,3584]{1,0:T(8,128)(2,1)}, u32[]{:S(2)}, u32[]{:S(2)}) collective-permute-start(bf16[80,3584]{1,0:T(8,128)(2,1)} %get-tuple-element.74), channel_id=1, source_target_pairs={{0,4},{1,5},{2,6},{3,7},{4,0},{5,1},{6,2},{7,3},{8,12},{9,13},{10,... | collective-permute-start | bytes 1720328 | tf_op jit(solution)/shard_map/ppermute | solution.py:25
  47.8 21.3 %collective-permute-start.8 = (bf16[80,3584]{1,0:T(8,128)(2,1)}, bf16[80,3584]{1,0:T(8,128)(2,1)}, u32[]{:S(2)}, u32[]{:S(2)}) collective-permute-start(bf16[80,3584]{1,0:T(8,128)(2,1)} %get-tuple-element.61), channel_id=1, source_target_pairs={{0,8},{1,9},{2,10},{3,11},{4,12},{5,13},{6,14},{7,15},{8,16},{9,17... | collective-permute-start | bytes 1720328 | tf_op jit(solution)/shard_map/ppermute | solution.py:25
  49.0 20.1 %collective-permute-start.9 = (bf16[80,3584]{1,0:T(8,128)(2,1)}, bf16[80,3584]{1,0:T(8,128)(2,1)}, u32[]{:S(2)}, u32[]{:S(2)}) collective-permute-start(bf16[80,3584]{1,0:T(8,128)(2,1)} %get-tuple-element.62), channel_id=1, source_target_pairs={{0,16},{1,17},{2,18},{3,19},{4,20},{5,21},{6,22},{7,23},{8,24},{9,... | collective-permute-start | bytes 1720328 | tf_op jit(solution)/shard_map/ppermute | solution.py:25
  49.8 26.8 %collective-permute-start.10 = (bf16[80,3584]{1,0:T(8,128)(2,1)}, bf16[80,3584]{1,0:T(8,128)(2,1)}, u32[]{:S(2)}, u32[]{:S(2)}) collective-permute-start(bf16[80,3584]{1,0:T(8,128)(2,1)} %get-tuple-element.63), channel_id=1, source_target_pairs={{0,24},{1,25},{2,26},{3,27},{4,28},{5,29},{6,30},{7,31},{8,0},{9,1... | collective-permute-start | bytes 1720328 | tf_op jit(solution)/shard_map/ppermute | solution.py:25
  69.0 21.4 %collective-permute-start.16 = (bf16[80,3584]{1,0:T(8,128)(2,1)}, bf16[80,3584]{1,0:T(8,128)(2,1)}, u32[]{:S(2)}, u32[]{:S(2)}) collective-permute-start(bf16[80,3584]{1,0:T(8,128)(2,1)} %collective-permute-done.14.refs_1_), channel_id=1, source_target_pairs={{0,2},{1,3},{2,0},{3,1},{4,6},{5,7},{6,4},{7,5},{8,10},{9,11},{10,... | collective-permute-start | bytes 1720328 | tf_op jit(solution)/shard_map/ppermute | solution.py:25
  86.0 15.3 %collective-permute-start.11 = (bf16[80,3584]{1,0:T(8,128)(2,1)}, bf16[80,3584]{1,0:T(8,128)(2,1)S(1)}, u32[]{:S(2)}, u32[]{:S(2)}) collective-permute-start(bf16[80,3584]{1,0:T(8,128)(2,1)} %get-tuple-element.65), channel_id=1, source_target_pairs={{0,24},{1,25},{2,26},{3,27},{4,28},{5,29},{6,30},{7,31},{8,0},{9,1... | collective-permute-start | bytes 1720328 | tf_op jit(solution)/shard_map/ppermute | solution.py:25
  86.1 26.6 %collective-permute-start.12 = (bf16[80,3584]{1,0:T(8,128)(2,1)}, bf16[80,3584]{1,0:T(8,128)(2,1)S(1)}, u32[]{:S(2)}, u32[]{:S(2)}) collective-permute-start(bf16[80,3584]{1,0:T(8,128)(2,1)} %get-tuple-element.66), channel_id=1, source_target_pairs={{0,16},{1,17},{2,18},{3,19},{4,20},{5,21},{6,22},{7,23},{8,24},{9,... | collective-permute-start | bytes 1720328 | tf_op jit(solution)/shard_map/ppermute | solution.py:25
  88.4 25.9 %collective-permute-start.13 = (bf16[80,3584]{1,0:T(8,128)(2,1)}, bf16[80,3584]{1,0:T(8,128)(2,1)S(1)}, u32[]{:S(2)}, u32[]{:S(2)}) collective-permute-start(bf16[80,3584]{1,0:T(8,128)(2,1)} %get-tuple-element.67), channel_id=1, source_target_pairs={{0,8},{1,9},{2,10},{3,11},{4,12},{5,13},{6,14},{7,15},{8,16},{9,17... | collective-permute-start | bytes 1720328 | tf_op jit(solution)/shard_map/ppermute | solution.py:25
  99.8 20.7 %collective-permute-start.17 = (bf16[80,3584]{1,0:T(8,128)(2,1)}, bf16[80,3584]{1,0:T(8,128)(2,1)S(1)}, u32[]{:S(2)}, u32[]{:S(2)}) collective-permute-start(bf16[80,3584]{1,0:T(8,128)(2,1)} %get-tuple-element.78), channel_id=1, source_target_pairs={{0,2},{1,3},{2,0},{3,1},{4,6},{5,7},{6,4},{7,5},{8,10},{9,11},{10,... | collective-permute-start | bytes 1720328 | tf_op jit(solution)/shard_map/ppermute | solution.py:25
  101.1 24.4 %collective-permute-start.18 = (bf16[80,3584]{1,0:T(8,128)(2,1)}, bf16[80,3584]{1,0:T(8,128)(2,1)S(1)}, u32[]{:S(2)}, u32[]{:S(2)}) collective-permute-start(bf16[80,3584]{1,0:T(8,128)(2,1)} %get-tuple-element.79), channel_id=1, source_target_pairs={{0,2},{1,3},{2,0},{3,1},{4,6},{5,7},{6,4},{7,5},{8,10},{9,11},{10,... | collective-permute-start | bytes 1720328 | tf_op jit(solution)/shard_map/ppermute | solution.py:25
  119.2 22.3 %collective-permute-start.20 = (bf16[64,3584]{1,0:T(8,128)(2,1)}, bf16[64,3584]{1,0:T(8,128)(2,1)S(1)}, u32[]{:S(2)}, u32[]{:S(2)}) collective-permute-start(bf16[64,3584]{1,0:T(8,128)(2,1)} %get-tuple-element.83), channel_id=1, source_target_pairs={{0,2},{1,3},{2,0},{3,1},{4,6},{5,7},{6,4},{7,5},{8,10},{9,11},{10,... | collective-permute-start | bytes 1376264 | tf_op jit(solution)/shard_map/ppermute | solution.py:25
  126.9 21.2 %collective-permute-start.22 = (bf16[80,3584]{1,0:T(8,128)(2,1)S(1)}, bf16[80,3584]{1,0:T(8,128)(2,1)S(1)}, u32[]{:S(2)}, u32[]{:S(2)}) collective-permute-start(bf16[80,3584]{1,0:T(8,128)(2,1)S(1)} %add_convert_fusion), channel_id=1, source_target_pairs={{0,4},{1,5},{2,6},{3,7},{4,0},{5,1},{6,2},{7,3},{8,12},{9,13},{10,... | collective-permute-start | bytes 1720328 | tf_op jit(solution)/shard_map/ppermute | solution.py:25
  128.7 35.0 %collective-permute-start.19 = (bf16[64,3584]{1,0:T(8,128)(2,1)}, bf16[64,3584]{1,0:T(8,128)(2,1)S(1)}, u32[]{:S(2)}, u32[]{:S(2)}) collective-permute-start(bf16[64,3584]{1,0:T(8,128)(2,1)} %get-tuple-element.81), channel_id=1, source_target_pairs={{0,2},{1,3},{2,0},{3,1},{4,6},{5,7},{6,4},{7,5},{8,10},{9,11},{10,... | collective-permute-start | bytes 1376264 | tf_op jit(solution)/shard_map/ppermute | solution.py:25
  155.0 19.7 %collective-permute-start.25 = (bf16[40,3584]{1,0:T(8,128)(2,1)}, bf16[40,3584]{1,0:T(8,128)(2,1)S(1)}, u32[]{:S(2)}, u32[]{:S(2)}) collective-permute-start(bf16[40,3584]{1,0:T(8,128)(2,1)} %get-tuple-element.94), channel_id=1, source_target_pairs={{0,16},{1,17},{2,18},{3,19},{4,20},{5,21},{6,22},{7,23},{8,24},{9,... | collective-permute-start | bytes 860168 | tf_op jit(solution)/shard_map/ppermute | solution.py:25
  155.6 19.2 %collective-permute-start.26 = (bf16[40,3584]{1,0:T(8,128)(2,1)}, bf16[40,3584]{1,0:T(8,128)(2,1)S(1)}, u32[]{:S(2)}, u32[]{:S(2)}) collective-permute-start(bf16[40,3584]{1,0:T(8,128)(2,1)} %get-tuple-element.95), channel_id=1, source_target_pairs={{0,8},{1,9},{2,10},{3,11},{4,12},{5,13},{6,14},{7,15},{8,16},{9,17... | collective-permute-start | bytes 860168 | tf_op jit(solution)/shard_map/ppermute | solution.py:25
  162.0 18.0 %collective-permute-start.24 = (bf16[64,1792]{1,0:T(8,128)(2,1)S(1)}, bf16[64,1792]{1,0:T(8,128)(2,1)S(1)}, u32[]{:S(2)}, u32[]{:S(2)}) collective-permute-start(bf16[64,1792]{1,0:T(8,128)(2,1)S(1)} %get-tuple-element.90), channel_id=1, source_target_pairs={{0,4},{1,5},{2,6},{3,7},{4,0},{5,1},{6,2},{7,3},{8,12},{9,13},{10,... | collective-permute-start | bytes 688136 | tf_op jit(solution)/shard_map/ppermute | solution.py:25
  163.9 45.2 %collective-permute-start.28 = (bf16[64,1792]{1,0:T(8,128)(2,1)S(1)}, bf16[64,1792]{1,0:T(8,128)(2,1)S(1)}, u32[]{:S(2)}, u32[]{:S(2)}) collective-permute-start(bf16[64,1792]{1,0:T(8,128)(2,1)S(1)} %fusion.3), channel_id=1, source_target_pairs={{32,0},{64,32},{96,64},{128,96},{160,128},{192,160},{224,192},{33,... | collective-permute-start | bytes 688136 | tf_op jit(solution)/shard_map/ppermute | solution.py:43
  178.1 30.1 %collective-permute-start.27 = (bf16[64,3584]{1,0:T(8,128)(2,1)}, bf16[64,3584]{1,0:T(8,128)(2,1)S(1)}, u32[]{:S(2)}, u32[]{:S(2)}) collective-permute-start(bf16[64,3584]{1,0:T(8,128)(2,1)} %shard_map.94), channel_id=1, source_target_pairs={{0,32},{32,64},{64,96},{96,128},{128,160},{160,192},{192,224},{1,3... | collective-permute-start | bytes 1376264 | tf_op jit(solution)/shard_map/ppermute | solution.py:43
  180.1 29.0 %collective-permute-start.29 = (bf16[64,1792]{1,0:T(8,128)(2,1)S(1)}, bf16[64,1792]{1,0:T(8,128)(2,1)S(1)}, u32[]{:S(2)}, u32[]{:S(2)}) collective-permute-start(bf16[64,1792]{1,0:T(8,128)(2,1)S(1)} %fusion.2), channel_id=1, source_target_pairs={{32,0},{64,32},{96,64},{128,96},{160,128},{192,160},{224,192},{33,... | collective-permute-start | bytes 688136 | tf_op jit(solution)/shard_map/ppermute | solution.py:43
  (22 other events, 322.2 us)

commit v3 on v1

--- a/solution.py
+++ b/solution.py
@@ -56,7 +56,7 @@
         kernel,
         out_shape=out_shape,
         cost_estimate=pl.CostEstimate(flops=1000, bytes_accessed=1000, transcendentals=0),
-        compiler_params=pltpu.CompilerParams(vmem_limit_bytes=60 * 1024 * 1024),
+        compiler_params=pltpu.CompilerParams(vmem_limit_bytes=63 * 1024 * 1024 + 512 * 1024),
         **kw,
     )
 

time: 210 us -> 209 us (level)
  other arithmetic: 6.11 us -> 10.3 us
  local copies, waits for them, and re-layouts: 4.07 us -> 0.7 us
    unnamed x36 -> x4, local copies, waits for them, and re-layouts: 4.07 us -> 0.7 us
    convert_element_type x4, other arithmetic: 4.35 us -> 6.65 us  [plus(): return (a.astype(jnp.float32) + b.astype(jnp.float32)).astype(jnp.bfloat16)]
  transfers between devices with their start and end apart: 30 -> 30, of which waited for: 13 -> 13; matrix products, arithmetic and copies ran while one was open for 3% -> 4% of each run, Pallas kernels for 19% -> 19%
where the time goes in v3:
time: 209 us; the launch traced here: 207 us
  waiting for transfers between devices  108 us (52%)
  starting transfers between devices  46.3 us (22%)
  Pallas kernels  40.9 us (20%)
  other arithmetic  10.3 us (5%)
    ppermute x27, waiting for transfers between devices, moved(): return lax.ppermute(block, 'expert', route)  92 us
    ppermute x27, starting transfers between devices, moved(): return lax.ppermute(block, 'expert', route)  30.2 us
    pallas_call x2, Pallas kernels, experts(): call(kernel, [shaped(slots, width)] * X, grid=(steps + down_steps,), in_s...  18.8 us
    ppermute x3, starting transfers between devices, shifted(): return lax.ppermute(block, 'section', route)  16.1 us
    ppermute x3, waiting for transfers between devices, shifted(): return lax.ppermute(block, 'section', route)  15.6 us
    convert_element_type x4, other arithmetic, plus(): return (a.astype(jnp.float32) + b.astype(jnp.float32)).astype(jnp.bfloat16)  6.65 us
    pallas_call x1, Pallas kernels, combine_line(): call(kernel, [shaped(rows, part, kind=jnp.float32)] * (2 * HALVES) + [sha...  5.03 us
  transfers between devices with their start and end apart: 30, of which 13 were waited for; matrix products, arithmetic and copies ran while one was open for 4% of the time, Pallas kernels for 19%

profile of v3, /device:TPU:195, one launch (start us, length us, event | category | flops | bytes accessed | tf_op | source)
XLA Modules:
  0.0 206.6 jit_solution(8603137172930779835)
XLA Ops:
  5.4 2.7 %shard_map.87 = (bf16[40,3584]{1,0:T(8,128)(2,1)}, bf16[40,3584]{1,0:T(8,128)(2,1)}, bf16[40,3584]{1,0:T(8,128)(2,1)}, bf16[40,3584]{1,0:T(8,128)(2,1)}, bf16[19...) custom-call(bf16[1,64,3584]{2,1,0:T(8,128)(2,1)} %refs_4_.5, f32[1,2,3584]{2,1,0:T(2,128)} %gain_ref.2, ...), custom_call_target="tpu_custom_call" | custom-call | flops 1000 | bytes 1000 | tf_op jit(solution)/shard_map/pallas_call | solution.py:173
  9.6 3.5 %collective-permute-done.4.refs_6_.refs_7_ = bf16[1,2,2,3584,256]{4,3,2,1,0:T(8,128)(2,1)} collective-permute-done((bf16[1,2,2,3584,256]{4,3,2,1,0:T(8,128)(2,1)}, bf16[1,2,2,3584,256]{4,3,2,1,0:T(8,128)(2,1)}, u32[]{:S(2)}, u32[]{:S(2)}) %collective-permute-start.4) | collective-permute-done | bytes 7340064 | tf_op jit(solution)/shard_map/ppermute | solution.py:25
  14.9 10.6 %collective-permute-done.refs_1_ = bf16[64,3712]{1,0:T(8,128)(2,1)} collective-permute-done((bf16[64,3712]{1,0:T(8,128)(2,1)}, bf16[64,3712]{1,0:T(8,128)(2,1)}, u32[]{:S(2)}, u32[]{:S(2)}) %collective-permute-start) | collective-permute-done | bytes 475168 | tf_op jit(solution)/shard_map/ppermute | solution.py:25
  27.6 2.7 %shard_map.88 = (bf16[80,3584]{1,0:T(8,128)(2,1)}, bf16[80,3584]{1,0:T(8,128)(2,1)}) custom-call(bf16[40,3584]{1,0:T(8,128)(2,1)} %get-tuple-element.54.refs_0_, bf16[40,3584]{1,0:T(8,128)(2,1)} %copy-done.1, bf16[40,3584]{1,0:T(8,128)(2,1)} %collective-permute-done.5.refs_2_, bf16[40,3584]{1,0:T(8,128)(2,1)} %collective-permute-done.6.refs_3_), custom_call_target="tpu_custom_call" | custom-call | flops 1000 | bytes 1000 | tf_op jit(solution)/shard_map/pallas_call | solution.py:231
  32.3 11.7 %collective-permute-done.2.refs_3_ = bf16[64,3712]{1,0:T(8,128)(2,1)} collective-permute-done((bf16[64,3712]{1,0:T(8,128)(2,1)}, bf16[64,3712]{1,0:T(8,128)(2,1)}, u32[]{:S(2)}, u32[]{:S(2)}) %collective-permute-start.2) | collective-permute-done | bytes 475168 | tf_op jit(solution)/shard_map/ppermute | solution.py:25
  45.9 3.9 %shard_map.89 = (bf16[80,3584]{1,0:T(8,128)(2,1)}, bf16[80,3584]{1,0:T(8,128)(2,1)}, bf16[80,3584]{1,0:T(8,128)(2,1)}, bf16[80,3584]{1,0:T(8,128)(2,1)}, bf16[32...) custom-call(bf16[64,3712]{1,0:T(8,128)(2,1)} %shard_map.86.refs_0_, bf16[64,3712]{1,0:T(8,128)(2,1)} %collective-permute-done.refs_1_, ...), custom_call_target="tpu_custom_call" | custom-call | flops 1000 | bytes 1000 | tf_op jit(solution)/shard_map/pallas_call | solution.py:197
  53.7 17.1 %collective-permute-done.17.refs_1_ = bf16[80,3584]{1,0:T(8,128)(2,1)} collective-permute-done((bf16[80,3584]{1,0:T(8,128)(2,1)}, bf16[80,3584]{1,0:T(8,128)(2,1)}, u32[]{:S(2)}, u32[]{:S(2)}) %collective-permute-start.17) | collective-permute-done | bytes 573472 | tf_op jit(solution)/shard_map/ppermute | solution.py:25
  70.8 2.7 %collective-permute-start.19 = (bf16[80,3584]{1,0:T(8,128)(2,1)}, bf16[80,3584]{1,0:T(8,128)(2,1)}, u32[]{:S(2)}, u32[]{:S(2)}) collective-permute-start(bf16[80,3584]{1,0:T(8,128)(2,1)} %collective-permute-done.17.refs_1_), channel_id=1, source_target_pairs={{0,2},{1,3},{2,0},{3,1},{4,6},{5,7},{6,4},{7,5},{8,10},{9,11},{10,... | collective-permute-start | bytes 1720328 | tf_op jit(solution)/shard_map/ppermute | solution.py:25
  73.5 5.1 %collective-permute-done.10.refs_3_ = bf16[80,3584]{1,0:T(8,128)(2,1)} collective-permute-done((bf16[80,3584]{1,0:T(8,128)(2,1)}, bf16[80,3584]{1,0:T(8,128)(2,1)}, u32[]{:S(2)}, u32[]{:S(2)}) %collective-permute-start.10) | collective-permute-done | bytes 573472 | tf_op jit(solution)/shard_map/ppermute | solution.py:25
  78.6 9.4 %shard_map.90 = (bf16[80,3584]{1,0:T(8,128)(2,1)}, bf16[80,3584]{1,0:T(8,128)(2,1)}, bf16[80,3584]{1,0:T(8,128)(2,1)}, bf16[80,3584]{1,0:T(8,128)(2,1)}) custom-call(bf16[80,3584]{1,0:T(8,128)(2,1)} %get-tuple-element.64.refs_0_, bf16[80,3584]{1,0:T(8,128)(2,1)} %collective-permute-done.8.refs_1_, bf16[80,3584]{1,0:T(8,128)(2,1)} %collective-permute-done.9.refs_2_, ...), custom_call_target="tpu_custom_call" | custom-call | flops 1000 | bytes 1000 | tf_op jit(solution)/shard_map/pallas_call | solution.py:309
  88.1 2.3 %collective-permute-start.12 = (bf16[80,3584]{1,0:T(8,128)(2,1)}, bf16[80,3584]{1,0:T(8,128)(2,1)}, u32[]{:S(2)}, u32[]{:S(2)}) collective-permute-start(bf16[80,3584]{1,0:T(8,128)(2,1)} %get-tuple-element.70), channel_id=1, source_target_pairs={{0,16},{1,17},{2,18},{3,19},{4,20},{5,21},{6,22},{7,23},{8,24},{9,... | collective-permute-start | bytes 1720328 | tf_op jit(solution)/shard_map/ppermute | solution.py:25
  92.4 9.4 %shard_map.92 = (bf16[80,3584]{1,0:T(8,128)(2,1)}, bf16[80,3584]{1,0:T(8,128)(2,1)}, bf16[80,3584]{1,0:T(8,128)(2,1)}, bf16[80,3584]{1,0:T(8,128)(2,1)}) custom-call(bf16[80,3584]{1,0:T(8,128)(2,1)} %get-tuple-element.79.refs_0_, bf16[80,3584]{1,0:T(8,128)(2,1)} %collective-permute-done.17.refs_1_, bf16[80,3584]{1,0:T(8,128)(2,1)} %collective-permute-done.18.refs_2_, ...), custom_call_target="tpu_custom_call" | custom-call | flops 1000 | bytes 1000 | tf_op jit(solution)/shard_map/pallas_call | solution.py:309
  103.3 11.4 %collective-permute-done.12.refs_2_ = bf16[80,3584]{1,0:T(8,128)(2,1)} collective-permute-done((bf16[80,3584]{1,0:T(8,128)(2,1)}, bf16[80,3584]{1,0:T(8,128)(2,1)}, u32[]{:S(2)}, u32[]{:S(2)}) %collective-permute-start.12) | collective-permute-done | bytes 573472 | tf_op jit(solution)/shard_map/ppermute | solution.py:25
  116.3 5.0 %shard_map.91 = (f32[64,1792]{1,0:T(8,128)}, f32[64,1792]{1,0:T(8,128)}, f32[64,1792]{1,0:T(8,128)}, f32[64,1792]{1,0:T(8,128)}, bf16[64,3584]{1,0:T(8,128)(2,1)}, /*index=5*/bf16[64,3584]{1,0:T(8,128)(2,1)}) custom-call(bf16[320,256]{1,0:T(8,128)(2,1)} %get-tuple-element.62.high_ref, bf16[320,256]{1,0:T(8,128)(2,1)} %get-tuple-element.63.low_ref, ...), custom_call_target="tpu_custom_call" | custom-call | flops 1000 | bytes 1000 | tf_op jit(solution)/shard_map/pallas_call | solution.py:364
  122.5 5.1 %collective-permute-done.21 = bf16[80,3584]{1,0:T(8,128)(2,1)} collective-permute-done((bf16[80,3584]{1,0:T(8,128)(2,1)}, bf16[80,3584]{1,0:T(8,128)(2,1)}, u32[]{:S(2)}, u32[]{:S(2)}) %collective-permute-start.21) | collective-permute-done | bytes 573472 | tf_op jit(solution)/shard_map/ppermute | solution.py:25
  131.0 12.5 %collective-permute-done.15 = bf16[64,3584]{1,0:T(8,128)(2,1)S(1)} collective-permute-done((bf16[64,3584]{1,0:T(8,128)(2,1)}, bf16[64,3584]{1,0:T(8,128)(2,1)S(1)}, u32[]{:S(2)}, u32[]{:S(2)}) %collective-permute-start.15) | collective-permute-done | bytes 458784 | tf_op jit(solution)/shard_map/ppermute | solution.py:25
  145.4 2.7 %collective-permute-start.16 = (bf16[64,1792]{1,0:T(8,128)(2,1)}, bf16[64,1792]{1,0:T(8,128)(2,1)}, u32[]{:S(2)}, u32[]{:S(2)}) collective-permute-start(bf16[64,1792]{1,0:T(8,128)(2,1)} %get-tuple-element.101), channel_id=1, source_target_pairs={{0,4},{1,5},{2,6},{3,7},{4,0},{5,1},{6,2},{7,3},{8,12},{9,13},{10,... | collective-permute-start | bytes 688136 | tf_op jit(solution)/shard_map/ppermute | solution.py:25
  148.1 2.1 %collective-permute-done.22.far_ref = bf16[80,3584]{1,0:T(8,128)(2,1)} collective-permute-done((bf16[80,3584]{1,0:T(8,128)(2,1)S(1)}, bf16[80,3584]{1,0:T(8,128)(2,1)}, u32[]{:S(2)}, u32[]{:S(2)}) %collective-permute-start.22) | collective-permute-done | bytes 573472 | tf_op jit(solution)/shard_map/ppermute | solution.py:25
  150.2 2.9 %shard_map.93 = (bf16[40,3584]{1,0:T(8,128)(2,1)}, bf16[40,3584]{1,0:T(8,128)(2,1)}, bf16[40,3584]{1,0:T(8,128)(2,1)}, bf16[40,3584]{1,0:T(8,128)(2,1)}) custom-call(bf16[80,3584]{1,0:T(8,128)(2,1)} %get-tuple-element.82.near_ref, bf16[80,3584]{1,0:T(8,128)(2,1)} %collective-permute-done.20.side_ref, bf16[80,3584]{1,0:T(8,128)(2,1)} %collective-permute-done.22.far_ref), custom_call_target="tpu_custom_call" | custom-call | flops 1000 | bytes 1000 | tf_op jit(solution)/shard_map/pallas_call | solution.py:252
  155.1 9.8 %collective-permute-done.16 = bf16[64,1792]{1,0:T(8,128)(2,1)} collective-permute-done((bf16[64,1792]{1,0:T(8,128)(2,1)}, bf16[64,1792]{1,0:T(8,128)(2,1)}, u32[]{:S(2)}, u32[]{:S(2)}) %collective-permute-start.16) | collective-permute-done | bytes 229408 | tf_op jit(solution)/shard_map/ppermute | solution.py:25
  167.0 4.8 %collective-permute-start.28 = (bf16[64,1792]{1,0:T(8,128)(2,1)}, bf16[64,1792]{1,0:T(8,128)(2,1)}, u32[]{:S(2)}, u32[]{:S(2)}) collective-permute-start(bf16[64,1792]{1,0:T(8,128)(2,1)} %fusion.3), channel_id=1, source_target_pairs={{32,0},{64,32},{96,64},{128,96},{160,128},{192,160},{224,192},{33,... | collective-permute-start | bytes 688136 | tf_op jit(solution)/shard_map/ppermute | solution.py:43
  171.9 2.8 %shard_map.94 = bf16[64,3584]{1,0:T(8,128)(2,1)} custom-call(bf16[192,64]{1,0:T(8,128)(2,1)} %get-tuple-element.92.high_ref, bf16[192,64]{1,0:T(8,128)(2,1)} %get-tuple-element.93.low_ref, bf16[40,3584]{1,0:T(8,128)(2,1)} %get-tuple-element.94.refs_0_, bf16[40,3584]{1,0:T(8,128)(2,1)} %collective-permute-done.24.refs_1_, ...), custom_call_target="tpu_custom_call" | custom-call | flops 1000 | bytes 1000 | tf_op jit(solution)/shard_map/pallas_call | solution.py:338
  177.9 9.4 %collective-permute-start.29 = (bf16[64,1792]{1,0:T(8,128)(2,1)S(1)}, bf16[64,1792]{1,0:T(8,128)(2,1)S(1)}, u32[]{:S(2)}, u32[]{:S(2)}) collective-permute-start(bf16[64,1792]{1,0:T(8,128)(2,1)S(1)} %fusion.2), channel_id=1, source_target_pairs={{32,0},{64,32},{96,64},{128,96},{160,128},{192,160},{224,192},{33,... | collective-permute-start | bytes 688136 | tf_op jit(solution)/shard_map/ppermute | solution.py:43
  187.3 15.6 %collective-permute-done.27 = bf16[64,3584]{1,0:T(8,128)(2,1)S(1)} collective-permute-done((bf16[64,3584]{1,0:T(8,128)(2,1)}, bf16[64,3584]{1,0:T(8,128)(2,1)S(1)}, u32[]{:S(2)}, u32[]{:S(2)}) %collective-permute-start.27) | collective-permute-done | bytes 458784 | tf_op jit(solution)/shard_map/ppermute | solution.py:43
  (55 shorter events, 40.7 us)
Async XLA Ops:
  3.5 22.0 %collective-permute-start = (bf16[64,3712]{1,0:T(8,128)(2,1)}, bf16[64,3712]{1,0:T(8,128)(2,1)}, u32[]{:S(2)}, u32[]{:S(2)}) collective-permute-start(bf16[64,3712]{1,0:T(8,128)(2,1)} %shard_map.86.refs_0_), channel_id=1, source_target_pairs={{0,4},{1,5},{2,6},{3,7},{4,0},{5,1},{6,2},{7,3},{8,12},{9,13},{10,... | collective-permute-start | bytes 1425416 | tf_op jit(solution)/shard_map/ppermute | solution.py:25
  4.6 22.3 %collective-permute-start.1 = (bf16[64,3712]{1,0:T(8,128)(2,1)}, bf16[64,3712]{1,0:T(8,128)(2,1)}, u32[]{:S(2)}, u32[]{:S(2)}) collective-permute-start(bf16[64,3712]{1,0:T(8,128)(2,1)} %shard_map.86.refs_0_), channel_id=1, source_target_pairs={{0,2},{1,3},{2,0},{3,1},{4,6},{5,7},{6,4},{7,5},{8,10},{9,11},{10,... | collective-permute-start | bytes 1425416 | tf_op jit(solution)/shard_map/ppermute | solution.py:25
  8.1 18.8 %collective-permute-start.3 = (bf16[40,3584]{1,0:T(8,128)(2,1)}, bf16[40,3584]{1,0:T(8,128)(2,1)S(1)}, u32[]{:S(2)}, u32[]{:S(2)}) collective-permute-start(bf16[40,3584]{1,0:T(8,128)(2,1)} %get-tuple-element.55), channel_id=1, source_target_pairs={{0,8},{1,9},{2,10},{3,11},{4,12},{5,13},{6,14},{7,15},{8,16},{9,17... | collective-permute-start | bytes 860168 | tf_op jit(solution)/shard_map/ppermute | solution.py:25
  9.3 17.6 %collective-permute-start.6 = (bf16[40,3584]{1,0:T(8,128)(2,1)}, bf16[40,3584]{1,0:T(8,128)(2,1)}, u32[]{:S(2)}, u32[]{:S(2)}) collective-permute-start(bf16[40,3584]{1,0:T(8,128)(2,1)} %get-tuple-element.58), channel_id=1, source_target_pairs={{0,24},{1,25},{2,26},{3,27},{4,28},{5,29},{6,30},{7,31},{8,0},{9,1... | collective-permute-start | bytes 860168 | tf_op jit(solution)/shard_map/ppermute | solution.py:25
  43.9 26.8 %collective-permute-start.17 = (bf16[80,3584]{1,0:T(8,128)(2,1)}, bf16[80,3584]{1,0:T(8,128)(2,1)}, u32[]{:S(2)}, u32[]{:S(2)}) collective-permute-start(bf16[80,3584]{1,0:T(8,128)(2,1)} %get-tuple-element.78), channel_id=1, source_target_pairs={{0,4},{1,5},{2,6},{3,7},{4,0},{5,1},{6,2},{7,3},{8,12},{9,13},{10,... | collective-permute-start | bytes 1720328 | tf_op jit(solution)/shard_map/ppermute | solution.py:25
  45.5 25.3 %collective-permute-start.18 = (bf16[80,3584]{1,0:T(8,128)(2,1)}, bf16[80,3584]{1,0:T(8,128)(2,1)}, u32[]{:S(2)}, u32[]{:S(2)}) collective-permute-start(bf16[80,3584]{1,0:T(8,128)(2,1)} %get-tuple-element.79.refs_0_), channel_id=1, source_target_pairs={{0,2},{1,3},{2,0},{3,1},{4,6},{5,7},{6,4},{7,5},{8,10},{9,11},{10,... | collective-permute-start | bytes 1720328 | tf_op jit(solution)/shard_map/ppermute | solution.py:25
  49.7 23.7 %collective-permute-start.8 = (bf16[80,3584]{1,0:T(8,128)(2,1)}, bf16[80,3584]{1,0:T(8,128)(2,1)}, u32[]{:S(2)}, u32[]{:S(2)}) collective-permute-start(bf16[80,3584]{1,0:T(8,128)(2,1)} %get-tuple-element.65), channel_id=1, source_target_pairs={{0,8},{1,9},{2,10},{3,11},{4,12},{5,13},{6,14},{7,15},{8,16},{9,17... | collective-permute-start | bytes 1720328 | tf_op jit(solution)/shard_map/ppermute | solution.py:25
  51.0 22.5 %collective-permute-start.9 = (bf16[80,3584]{1,0:T(8,128)(2,1)}, bf16[80,3584]{1,0:T(8,128)(2,1)}, u32[]{:S(2)}, u32[]{:S(2)}) collective-permute-start(bf16[80,3584]{1,0:T(8,128)(2,1)} %get-tuple-element.66), channel_id=1, source_target_pairs={{0,16},{1,17},{2,18},{3,19},{4,20},{5,21},{6,22},{7,23},{8,24},{9,... | collective-permute-start | bytes 1720328 | tf_op jit(solution)/shard_map/ppermute | solution.py:25
  51.8 26.8 %collective-permute-start.10 = (bf16[80,3584]{1,0:T(8,128)(2,1)}, bf16[80,3584]{1,0:T(8,128)(2,1)}, u32[]{:S(2)}, u32[]{:S(2)}) collective-permute-start(bf16[80,3584]{1,0:T(8,128)(2,1)} %get-tuple-element.67), channel_id=1, source_target_pairs={{0,24},{1,25},{2,26},{3,27},{4,28},{5,29},{6,30},{7,31},{8,0},{9,1... | collective-permute-start | bytes 1720328 | tf_op jit(solution)/shard_map/ppermute | solution.py:25
  70.8 21.6 %collective-permute-start.19 = (bf16[80,3584]{1,0:T(8,128)(2,1)}, bf16[80,3584]{1,0:T(8,128)(2,1)}, u32[]{:S(2)}, u32[]{:S(2)}) collective-permute-start(bf16[80,3584]{1,0:T(8,128)(2,1)} %collective-permute-done.17.refs_1_), channel_id=1, source_target_pairs={{0,2},{1,3},{2,0},{3,1},{4,6},{5,7},{6,4},{7,5},{8,10},{9,11},{10,... | collective-permute-start | bytes 1720328 | tf_op jit(solution)/shard_map/ppermute | solution.py:25
  88.1 26.7 %collective-permute-start.12 = (bf16[80,3584]{1,0:T(8,128)(2,1)}, bf16[80,3584]{1,0:T(8,128)(2,1)}, u32[]{:S(2)}, u32[]{:S(2)}) collective-permute-start(bf16[80,3584]{1,0:T(8,128)(2,1)} %get-tuple-element.70), channel_id=1, source_target_pairs={{0,16},{1,17},{2,18},{3,19},{4,20},{5,21},{6,22},{7,23},{8,24},{9,... | collective-permute-start | bytes 1720328 | tf_op jit(solution)/shard_map/ppermute | solution.py:25
  90.4 25.9 %collective-permute-start.13 = (bf16[80,3584]{1,0:T(8,128)(2,1)}, bf16[80,3584]{1,0:T(8,128)(2,1)}, u32[]{:S(2)}, u32[]{:S(2)}) collective-permute-start(bf16[80,3584]{1,0:T(8,128)(2,1)} %get-tuple-element.71), channel_id=1, source_target_pairs={{0,8},{1,9},{2,10},{3,11},{4,12},{5,13},{6,14},{7,15},{8,16},{9,17... | collective-permute-start | bytes 1720328 | tf_op jit(solution)/shard_map/ppermute | solution.py:25
  101.8 20.7 %collective-permute-start.20 = (bf16[80,3584]{1,0:T(8,128)(2,1)}, bf16[80,3584]{1,0:T(8,128)(2,1)}, u32[]{:S(2)}, u32[]{:S(2)}) collective-permute-start(bf16[80,3584]{1,0:T(8,128)(2,1)} %get-tuple-element.83), channel_id=1, source_target_pairs={{0,2},{1,3},{2,0},{3,1},{4,6},{5,7},{6,4},{7,5},{8,10},{9,11},{10,... | collective-permute-start | bytes 1720328 | tf_op jit(solution)/shard_map/ppermute | solution.py:25
  103.0 24.6 %collective-permute-start.21 = (bf16[80,3584]{1,0:T(8,128)(2,1)}, bf16[80,3584]{1,0:T(8,128)(2,1)}, u32[]{:S(2)}, u32[]{:S(2)}) collective-permute-start(bf16[80,3584]{1,0:T(8,128)(2,1)} %get-tuple-element.85), channel_id=1, source_target_pairs={{0,2},{1,3},{2,0},{3,1},{4,6},{5,7},{6,4},{7,5},{8,10},{9,11},{10,... | collective-permute-start | bytes 1720328 | tf_op jit(solution)/shard_map/ppermute | solution.py:25
  121.4 22.1 %collective-permute-start.15 = (bf16[64,3584]{1,0:T(8,128)(2,1)}, bf16[64,3584]{1,0:T(8,128)(2,1)S(1)}, u32[]{:S(2)}, u32[]{:S(2)}) collective-permute-start(bf16[64,3584]{1,0:T(8,128)(2,1)} %get-tuple-element.75), channel_id=1, source_target_pairs={{0,2},{1,3},{2,0},{3,1},{4,6},{5,7},{6,4},{7,5},{8,10},{9,11},{10,... | collective-permute-start | bytes 1376264 | tf_op jit(solution)/shard_map/ppermute | solution.py:25
  129.0 21.2 %collective-permute-start.22 = (bf16[80,3584]{1,0:T(8,128)(2,1)S(1)}, bf16[80,3584]{1,0:T(8,128)(2,1)}, u32[]{:S(2)}, u32[]{:S(2)}) collective-permute-start(bf16[80,3584]{1,0:T(8,128)(2,1)S(1)} %add_convert_fusion), channel_id=1, source_target_pairs={{0,4},{1,5},{2,6},{3,7},{4,0},{5,1},{6,2},{7,3},{8,12},{9,13},{10,... | collective-permute-start | bytes 1720328 | tf_op jit(solution)/shard_map/ppermute | solution.py:25
  130.6 34.4 %collective-permute-start.14 = (bf16[64,3584]{1,0:T(8,128)(2,1)}, bf16[64,3584]{1,0:T(8,128)(2,1)}, u32[]{:S(2)}, u32[]{:S(2)}) collective-permute-start(bf16[64,3584]{1,0:T(8,128)(2,1)} %get-tuple-element.73), channel_id=1, source_target_pairs={{0,2},{1,3},{2,0},{3,1},{4,6},{5,7},{6,4},{7,5},{8,10},{9,11},{10,... | collective-permute-start | bytes 1376264 | tf_op jit(solution)/shard_map/ppermute | solution.py:25
  145.4 19.6 %collective-permute-start.16 = (bf16[64,1792]{1,0:T(8,128)(2,1)}, bf16[64,1792]{1,0:T(8,128)(2,1)}, u32[]{:S(2)}, u32[]{:S(2)}) collective-permute-start(bf16[64,1792]{1,0:T(8,128)(2,1)} %get-tuple-element.101), channel_id=1, source_target_pairs={{0,4},{1,5},{2,6},{3,7},{4,0},{5,1},{6,2},{7,3},{8,12},{9,13},{10,... | collective-permute-start | bytes 688136 | tf_op jit(solution)/shard_map/ppermute | solution.py:25
  153.1 18.7 %collective-permute-start.24 = (bf16[40,3584]{1,0:T(8,128)(2,1)}, bf16[40,3584]{1,0:T(8,128)(2,1)}, u32[]{:S(2)}, u32[]{:S(2)}) collective-permute-start(bf16[40,3584]{1,0:T(8,128)(2,1)} %get-tuple-element.95), channel_id=1, source_target_pairs={{0,24},{1,25},{2,26},{3,27},{4,28},{5,29},{6,30},{7,31},{8,0},{9,1... | collective-permute-start | bytes 860168 | tf_op jit(solution)/shard_map/ppermute | solution.py:25
  153.5 18.4 %collective-permute-start.25 = (bf16[40,3584]{1,0:T(8,128)(2,1)}, bf16[40,3584]{1,0:T(8,128)(2,1)}, u32[]{:S(2)}, u32[]{:S(2)}) collective-permute-start(bf16[40,3584]{1,0:T(8,128)(2,1)} %get-tuple-element.96), channel_id=1, source_target_pairs={{0,16},{1,17},{2,18},{3,19},{4,20},{5,21},{6,22},{7,23},{8,24},{9,... | collective-permute-start | bytes 860168 | tf_op jit(solution)/shard_map/ppermute | solution.py:25
  154.2 17.7 %collective-permute-start.26 = (bf16[40,3584]{1,0:T(8,128)(2,1)}, bf16[40,3584]{1,0:T(8,128)(2,1)}, u32[]{:S(2)}, u32[]{:S(2)}) collective-permute-start(bf16[40,3584]{1,0:T(8,128)(2,1)} %get-tuple-element.97), channel_id=1, source_target_pairs={{0,8},{1,9},{2,10},{3,11},{4,12},{5,13},{6,14},{7,15},{8,16},{9,17... | collective-permute-start | bytes 860168 | tf_op jit(solution)/shard_map/ppermute | solution.py:25
  167.0 37.8 %collective-permute-start.28 = (bf16[64,1792]{1,0:T(8,128)(2,1)}, bf16[64,1792]{1,0:T(8,128)(2,1)}, u32[]{:S(2)}, u32[]{:S(2)}) collective-permute-start(bf16[64,1792]{1,0:T(8,128)(2,1)} %fusion.3), channel_id=1, source_target_pairs={{32,0},{64,32},{96,64},{128,96},{160,128},{192,160},{224,192},{33,... | collective-permute-start | bytes 688136 | tf_op jit(solution)/shard_map/ppermute | solution.py:43
  174.7 28.2 %collective-permute-start.27 = (bf16[64,3584]{1,0:T(8,128)(2,1)}, bf16[64,3584]{1,0:T(8,128)(2,1)S(1)}, u32[]{:S(2)}, u32[]{:S(2)}) collective-permute-start(bf16[64,3584]{1,0:T(8,128)(2,1)} %shard_map.94), channel_id=1, source_target_pairs={{0,32},{32,64},{64,96},{96,128},{128,160},{160,192},{192,224},{1,3... | collective-permute-start | bytes 1376264 | tf_op jit(solution)/shard_map/ppermute | solution.py:43
  177.9 26.8 %collective-permute-start.29 = (bf16[64,1792]{1,0:T(8,128)(2,1)S(1)}, bf16[64,1792]{1,0:T(8,128)(2,1)S(1)}, u32[]{:S(2)}, u32[]{:S(2)}) collective-permute-start(bf16[64,1792]{1,0:T(8,128)(2,1)S(1)} %fusion.2), channel_id=1, source_target_pairs={{32,0},{64,32},{96,64},{128,96},{160,128},{192,160},{224,192},{33,... | collective-permute-start | bytes 688136 | tf_op jit(solution)/shard_map/ppermute | solution.py:43
  (8 other events, 131.0 us)
